TPU v7x, 512 devices: a whole 4x4x16 slice. The times are simulated.
512 devices in a mesh: grp: 4 (over z_hi, core), seq: 32 (over y, z_lo), tp: 4 (over x).
Axes of the slice: x: 4, y: 4, z: 16 (z_hi: 2, z_lo: 8; z = z_hi * 8 + z_lo), core: 2. Of those that a mesh axis runs over, the one named last changes fastest.
Arguments:
- student_hidden_states: bfloat16 [4096, 5120], P('seq'), may hold values from -6 to 6
- student_norm_gain: float32 [5120], replicated, may hold values from 0.25 to 1.75
- student_output_head: bfloat16 [5120, 64], replicated, may hold values from -0.078125 to 0.078125
- noise: bfloat16 [4096, 64], P('seq'), may hold values from -6 to 6
- timestep: int32 [1], replicated, may hold values from 20 to 979
- context: bfloat16 [4096, 5120], P('seq'), may hold values from -80 to 80
- patch_embedding_input: bfloat16 [64, 5120], replicated, may hold values from -0.75 to 0.75
- attention_norm_gain: float32 [5120], replicated, may hold values from 0.25 to 1.75
- query_weight: bfloat16 [5120, 4096], P('seq', ('grp', 'tp')), may hold values from -1 to 1
- key_weight: bfloat16 [5120, 4096], P('seq', ('grp', 'tp')), may hold values from -1 to 1
- value_weight: bfloat16 [5120, 4096], P('seq', ('grp', 'tp')), may hold values from -0.078125 to 0.078125
- adapter_down_weight: bfloat16 [5120, 64], P('seq'), may hold values from -0.078125 to 0.078125
- adapter_up_weight: bfloat16 [64, 4096], P(None, ('grp', 'tp')), may hold values from -0.75 to 0.75
- output_weight: bfloat16 [4096, 5120], P(('grp', 'tp'), 'seq'), may hold values from -0.09375 to 0.09375
- velocity_head_output: bfloat16 [5120, 64], replicated, may hold values from -0.078125 to 0.078125
Outputs:
- dmd_grad: float32 [4096, 64], P('seq')
- head_grad: float32 [5120, 64], P(('grp', 'tp'))
All inputs are finite; a program needn't handle non-finite values. Where the computation divides by a largest or mean magnitude, that divisor is 1e-20 or more.
Results may differ from a plain program's by a relative error of at most 0.015.
The roundings to bfloat16 on the way count: a program that leaves them out, or rounds other values in their place, can miss the bound.
Values may be sent and summed in bfloat16 or wider, within the bound.
A program may use at most 64 MiB of HBM per device.

v0:
```python
import jax
import jax.numpy as jnp
from jax import lax
from jax.sharding import PartitionSpec as P

HEAD_WIDTH = 128
LAT = 64


def rms_norm(values):
    return values * lax.rsqrt(jnp.mean(values * values, axis=-1, keepdims=True) + 1e-06)


def local(
    student_hidden_states,
    student_norm_gain,
    student_output_head,
    noise,
    timestep,
    context,
    patch_embedding_input,
    attention_norm_gain,
    query_weight,
    key_weight,
    value_weight,
    adapter_down_weight,
    adapter_up_weight,
    output_weight,
    velocity_head_output,
):
    tokens = noise.shape[0]
    local_cols = query_weight.shape[1]
    local_heads = local_cols // HEAD_WIDTH
    fraction = timestep[0].astype(jnp.float32) / 1000.0
    noise_level = 5.0 * fraction / (1.0 + 4.0 * fraction)
    act_student = (rms_norm(student_hidden_states.astype(jnp.float32)) * student_norm_gain).astype(
        jnp.bfloat16
    )
    latent = jnp.dot(act_student, student_output_head, preferred_element_type=jnp.float32)
    noisy = ((1.0 - noise_level) * latent + noise_level * noise.astype(jnp.float32)).astype(
        jnp.bfloat16
    )
    hidden = jnp.dot(
        noisy, patch_embedding_input, preferred_element_type=jnp.float32
    ) + context.astype(jnp.float32)
    activation = (rms_norm(hidden) * attention_norm_gain).astype(jnp.bfloat16)
    blocks = (
        lax.all_gather(query_weight, "seq", axis=0, tiled=True),
        lax.all_gather(key_weight, "seq", axis=0, tiled=True),
        lax.all_gather(value_weight, "seq", axis=0, tiled=True),
        lax.all_gather(adapter_down_weight, "seq", axis=0, tiled=True),
    )
    complete_query, key_full, value_full, low_full = tuple(
        (jnp.dot(activation, block, preferred_element_type=jnp.float32) for block in blocks)
    )
    adapter_lowrank = low_full.astype(jnp.bfloat16)
    q_teacher = complete_query.astype(jnp.bfloat16)
    fake_query_rows = (
        complete_query
        + jnp.dot(adapter_lowrank, adapter_up_weight, preferred_element_type=jnp.float32)
    ).astype(jnp.bfloat16)
    keys = key_full.astype(jnp.bfloat16)
    values = value_full.astype(jnp.bfloat16)
    queries = jnp.stack([q_teacher, fake_query_rows]).reshape(2, tokens, local_heads, HEAD_WIDTH)
    blocks = (
        lax.all_gather(keys, "seq", axis=0, tiled=True),
        lax.all_gather(values, "seq", axis=0, tiled=True),
    )
    running_max = jnp.full((2, local_heads, tokens), -1e30, jnp.float32)
    key_rows = blocks[0].reshape(blocks[0].shape[0], local_heads, HEAD_WIDTH)
    value_rows = blocks[1].reshape(blocks[1].shape[0], local_heads, HEAD_WIDTH)
    scores = jnp.einsum(
        "mqhd,khd->mhqk", queries, key_rows, preferred_element_type=jnp.float32
    ) * HEAD_WIDTH ** (-0.5)
    new_max = jnp.maximum(running_max, jnp.max(scores, axis=-1))
    expo = jnp.exp(scores - new_max[..., None])
    new_sum = jnp.sum(expo, axis=-1)
    update = jnp.einsum(
        "mhqk,khd->mhqd", expo.astype(jnp.bfloat16), value_rows, preferred_element_type=jnp.float32
    )
    attended = (update / new_sum[..., None]).astype(jnp.bfloat16)
    attended = attended.transpose(0, 2, 1, 3).reshape(2, tokens, local_cols)
    branch = jnp.einsum(
        "mqc,cn->mqn",
        attended,
        lax.all_gather(output_weight, "seq", axis=1, tiled=True),
        preferred_element_type=jnp.float32,
    )
    head_rows = velocity_head_output.astype(jnp.float32)
    shares = jnp.einsum("mqn,ne->mqe", branch, head_rows, precision=lax.Precision.HIGHEST)
    share_teacher, share_fake = lax.psum((shares[0], shares[1]), ("grp", "tp"))
    residual_part = jnp.dot(
        hidden, velocity_head_output.astype(jnp.float32), precision=lax.Precision.HIGHEST
    )
    noisy_float = noisy.astype(jnp.float32)
    real_pred = noisy_float - noise_level * (residual_part + share_teacher)
    fake_pred = noisy_float - noise_level * (residual_part + share_fake)
    diff = fake_pred - real_pred
    gap_part = jnp.sum(jnp.abs(latent - real_pred))
    row_block = student_output_head.shape[0] // (lax.axis_size("grp") * lax.axis_size("tp"))
    row_start = (lax.axis_index("grp") * lax.axis_size("tp") + lax.axis_index("tp")) * row_block
    act_block = lax.dynamic_slice_in_dim(act_student, row_start, row_block, 1).astype(jnp.float32)
    grad_part = jnp.einsum("td,te->de", act_block, diff, precision=lax.Precision.HIGHEST)
    grad_total, gap_total = lax.psum((grad_part, gap_part), "seq")
    all_tokens = tokens * lax.axis_size("seq")
    count = all_tokens * LAT
    norm_scale = 1.0 / (gap_total / count + 1e-05)
    token_scale = 1.0 / jnp.sqrt(jnp.float32(all_tokens))
    return (norm_scale * diff, norm_scale * token_scale * grad_total)


def solution(mesh):
    in_specs = (
        P("seq", None),
        P(),
        P(),
        P("seq", None),
        P(),
        P("seq", None),
        P(),
        P(),
        P("seq", ("grp", "tp")),
        P("seq", ("grp", "tp")),
        P("seq", ("grp", "tp")),
        P("seq", None),
        P(None, ("grp", "tp")),
        P(("grp", "tp"), "seq"),
        P(),
    )
    out_specs = (P("seq", None), P(("grp", "tp"), None))
    return jax.shard_map(local, mesh=mesh, in_specs=in_specs, out_specs=out_specs, check_vma=False)
```

profile of v0, /device:TPU:24, one launch (start us, length us, event | category | flops | bytes accessed | tf_op | source)
XLA Modules:
  0.0 2167.0 jit_solution(682647427826460014)
XLA Ops:
  7.2 0.0 all-gather.12.cloned.1.call-start
  7.2 0.7 all-gather.12.cloned.1.call-update
  7.9 0.0 all-gather.8.cloned.1.call-start
  8.0 0.7 all-gather.8.cloned.1.call-update
  8.7 0.0 all-gather.16.cloned.1.call-start
  8.7 0.7 all-gather.16.cloned.1.call-update
  9.4 0.0 all-gather.14.cloned.1.call-start
  10.2 1.7 fusion.7
  11.8 1.8 fusion.9
  13.7 0.6 add_convert_fusion
  14.3 0.6 multiply_reduce_fusion
  15.0 1.5 copy-done.1
  16.5 0.3 multiply_convert_fusion
  16.8 209.5 %all-gather.12.cloned.1.call-done = bf16[5120,256]{1,0:T(8,128)(2,1)} async-done(((bf16[160,256]{1,0:T(8,128)(2,1)}), bf16[5120,256]{1,0:T(8,128)(2,1)}) %all-gather.12.cloned.1.call-update) | async-done | bytes 2621456 | tf_op jit(solution)/shard_map/all_gather | solution.py:49
  226.3 2.9 convolution_convert_fusion
  229.2 0.0 all-gather.14.cloned.1.call-update
  229.2 0.0 all-gather.10.cloned.1.call-start
  229.3 227.7 %all-gather.8.cloned.1.call-done = bf16[5120,256]{1,0:T(8,128)(2,1)} async-done(((bf16[160,256]{1,0:T(8,128)(2,1)}), bf16[5120,256]{1,0:T(8,128)(2,1)}) %all-gather.8.cloned.1.call-update) | async-done | bytes 2621456 | tf_op jit(solution)/shard_map/all_gather | solution.py:50
  456.9 2.9 convolution_convert_fusion.1
  459.8 0.0 all-gather.10.cloned.1.call-update
  459.8 0.0 all-gather.18.cloned.1.call-start
  459.9 0.5 all-gather.18.cloned.1.call-update
  460.4 0.0 all-reduce.6.cloned.1.call-start
  460.5 124.5 %all-gather = bf16[32,160,64]{1,2,0:T(8,128)(2,1)S(1)} all-gather(bf16[1,160,64]{1,2,0:T(8,128)(2,1)S(1)} %bitcast.66), channel_id=1, replica_groups=mesh['grp'=4,'seq'=32,'tp'=4] {'seq'}, dimensions={0}, use_global_device_ids=true | all-gather | bytes 675840 | tf_op jit(solution)/shard_map/all_gather | solution.py:51
  584.9 0.6 copy.29
  585.5 2.5 reshape.52
  588.1 99.8 %all-gather.16.cloned.1.call-done = bf16[5120,256]{1,0:T(8,128)(2,1)} async-done(((bf16[160,256]{1,0:T(8,128)(2,1)}), bf16[5120,256]{1,0:T(8,128)(2,1)}) %all-gather.16.cloned.1.call-update) | async-done | bytes 2621456 | tf_op jit(solution)/shard_map/all_gather | solution.py:48
  687.8 2.2 fusion.36
  690.1 0.8 fusion.17
  691.0 224.6 %all-gather.14.cloned.1.call-done = bf16[4096,256]{1,0:T(8,128)(2,1)} async-done(((bf16[128,256]{1,0:T(8,128)(2,1)}), bf16[4096,256]{1,0:T(8,128)(2,1)}) %all-gather.14.cloned.1.call-update) | async-done | bytes 2097168 | tf_op jit(solution)/shard_map/all_gather | solution.py:66
  915.7 4.0 reshape.49
  919.6 223.9 %all-gather.10.cloned.1.call-done = bf16[4096,256]{1,0:T(8,128)(2,1)} async-done(((bf16[128,256]{1,0:T(8,128)(2,1)}), bf16[4096,256]{1,0:T(8,128)(2,1)}) %all-gather.10.cloned.1.call-update) | async-done | bytes 2097168 | tf_op jit(solution)/shard_map/all_gather | solution.py:67
  1143.5 2.9 copy.41
  1146.4 2.8 bitcast_reduce_fusion
  1149.3 1.4 fusion.1
  1150.7 1.6 fusion.21
  1152.3 221.4 %all-gather.18.cloned.1.call-done = bf16[256,5120]{0,1:T(8,128)(2,1)} async-done(((bf16[256,160]{0,1:T(8,128)(2,1)}), bf16[256,5120]{0,1:T(8,128)(2,1)}) %all-gather.18.cloned.1.call-update) | async-done | bytes 2621456 | tf_op jit(solution)/shard_map/all_gather | solution.py:86
  1373.7 2.7 fusion.10
  1376.5 2.8 fusion.24
  1379.3 0.6 slice_bitcast_fusion.1
  1380.0 0.0 all-reduce.4.cloned.1.call-start
  1380.0 259.8 %all-reduce.6.cloned.1.call-done = (f32[128,64]{0,1:T(8,128)}, f32[128,64]{0,1:T(8,128)}) async-done(((f32[128,64]{0,1:T(8,128)}, f32[128,64]{0,1:T(8,128)}), (f32[128,64]{0,1:T(8,128)}, f32[128,64]{0,1:T(8,128)})) %all-reduce.6.cloned.1.call-update) | async-done | bytes 65552 | tf_op jit(solution)/shard_map/psum | solution.py:91
  1639.8 3.4 abs_reduce_fusion
  1643.1 113.1 %psum.29 = f32[]{:T(128)} all-reduce(f32[]{:T(128)} %get-tuple-element.16), channel_id=1, replica_groups=mesh['grp'=4,'seq'=32,'tp'=4] {'seq'}, use_global_device_ids=true, to_apply=%region_6.0 | all-reduce | flops 1 | bytes 8 | tf_op jit(solution)/shard_map/psum | solution.py:104
  1756.9 0.6 broadcast_multiply_fusion.1
  1757.5 1.8 fusion.29
  1759.4 399.2 %all-reduce.4.cloned.1.call-done = f32[320,64]{0,1:T(8,128)} async-done(((f32[320,64]{0,1:T(8,128)}), f32[320,64]{0,1:T(8,128)}) %all-reduce.4.cloned.1.call-update) | async-done | bytes 81936 | tf_op jit(solution)/shard_map/psum | solution.py:104
  2158.6 1.5 broadcast_multiply_fusion
  (37 shorter events, 0.2 us)
Async XLA Ops:
  7.2 7.1 copy-start
  7.2 6.5 copy-start.7
  7.2 6.5 copy-start.13
  7.2 219.1 %all-gather.12.cloned.1.call-start = ((), (), s32[]{:S(2)}) async-start(), calls=%async_computation.2 | async-start | bytes 2703360 | tf_op jit(solution)/shard_map/all_gather | solution.py:49
  7.9 449.0 %all-gather.8.cloned.1.call-start = ((), (), s32[]{:S(2)}) async-start(), calls=%async_computation | async-start | bytes 2703360 | tf_op jit(solution)/shard_map/all_gather | solution.py:50
  8.7 679.1 %all-gather.16.cloned.1.call-start = ((), (), s32[]{:S(2)}) async-start(), calls=%async_computation.4 | async-start | bytes 2703360 | tf_op jit(solution)/shard_map/all_gather | solution.py:48
  9.4 906.2 %all-gather.14.cloned.1.call-start = ((), (), s32[]{:S(2)}) async-start(), calls=%async_computation.3 | async-start | bytes 2162688 | tf_op jit(solution)/shard_map/all_gather | solution.py:66
  11.8 2.5 copy-start.6
  13.7 1.3 copy-start.3
  14.3 2.2 copy-start.12
  15.0 1.5 copy-start.1
  229.2 231.3 %copy-start.10 = (bf16[160,64]{0,1:T(8,128)(2,1)S(1)}, bf16[160,64]{0,1:T(8,128)(2,1)}, u32[]{:S(2)}) copy-start(bf16[160,64]{0,1:T(8,128)(2,1)} %param.26) | copy-start | bytes 61444
  229.2 914.3 %all-gather.10.cloned.1.call-start = ((), (), s32[]{:S(2)}) async-start(), calls=%async_computation.1 | async-start | bytes 2162688 | tf_op jit(solution)/shard_map/all_gather | solution.py:67
  459.8 913.9 %all-gather.18.cloned.1.call-start = ((), (), s32[]{:S(2)}) async-start(), calls=%async_computation.5 | async-start | bytes 2703360 | tf_op jit(solution)/shard_map/all_gather | solution.py:86
  460.4 1179.4 %all-reduce.6.cloned.1.call-start = ((), (), s32[]{:S(2)}) async-start(), calls=%async_computation.7 | async-start | bytes 131072 | tf_op jit(solution)/shard_map/psum | solution.py:91
  585.5 104.6 %copy-start.9 = (bf16[64,256]{1,0:T(8,128)(2,1)S(1)}, bf16[64,256]{1,0:T(8,128)(2,1)}, u32[]{:S(2)}) copy-start(bf16[64,256]{1,0:T(8,128)(2,1)} %param.27) | copy-start | bytes 98308
  588.1 102.0 %copy-start.5 = (bf16[5120,64]{0,1:T(8,128)(2,1)S(1)}, bf16[5120,64]{0,1:T(8,128)(2,1)}, u32[]{:S(2)}) copy-start(bf16[5120,64]{0,1:T(8,128)(2,1)} %reshape.52) | copy-start | bytes 1966084
  1373.7 2.7 copy-start.4
  1376.5 263.3 %copy-start.2 = (f32[128,5120]{1,0:T(8,128)S(1)}, f32[128,5120]{1,0:T(8,128)}, u32[]{:S(2)}) copy-start(f32[128,5120]{1,0:T(8,128)} %copy-done.1) | copy-start | bytes 7864324
  1380.0 778.7 %all-reduce.4.cloned.1.call-start = ((), (), s32[]{:S(2)}) async-start(), calls=%async_computation.6 | async-start | bytes 196608 | tf_op jit(solution)/shard_map/psum | solution.py:104
  1639.8 117.1 %copy-start.8 = (f32[128,64]{0,1:T(8,128)S(1)}, f32[128,64]{0,1:T(8,128)}, u32[]{:S(2)}) copy-start(f32[128,64]{0,1:T(8,128)} %get-tuple-element.3) | copy-start | bytes 98308
  1639.8 117.1 %copy-start.11 = (f32[128,64]{0,1:T(8,128)S(1)}, f32[128,64]{0,1:T(8,128)}, u32[]{:S(2)}) copy-start(f32[128,64]{0,1:T(8,128)} %get-tuple-element.2) | copy-start | bytes 98308
Sparse Core Ops, SparseCore 0:
  10.1 216.1 all-gather.11
  228.4 228.4 all-gather.7
  459.0 228.7 all-gather.15
  689.8 225.8 all-gather.13
  918.2 225.3 all-gather.9
  1145.5 228.2 all-gather.17
  1380.1 259.6 all-reduce.5
  1759.5 399.0 all-reduce.3
where the time goes:
time: 2180 us; the launch traced here: 2170 us
  waiting for transfers between devices  1870 us (86%)
  blocking collectives  238 us (11%)
  matrix products  25.2 us (1%)
    psum x1, waiting for transfers between devices, local(): grad_total, gap_total = lax.psum((grad_part, gap_part), 'seq')  399 us
    psum x1, waiting for transfers between devices, local(): share_teacher, share_fake = lax.psum((shares[0], shares[1]), ('grp', 'tp'))  260 us
    all_gather x1, waiting for transfers between devices, local(): lax.all_gather(value_weight, 'seq', axis=0, tiled=True)  228 us
    all_gather x1, waiting for transfers between devices, local(): lax.all_gather(keys, 'seq', axis=0, tiled=True)  225 us
    all_gather x1, waiting for transfers between devices, local(): lax.all_gather(values, 'seq', axis=0, tiled=True)  224 us
    all_gather x1, waiting for transfers between devices, local(): lax.all_gather(output_weight, 'seq', axis=1, tiled=True)  221 us
    all_gather x1, waiting for transfers between devices, local(): lax.all_gather(key_weight, 'seq', axis=0, tiled=True)  210 us
    all_gather x1, blocking collectives, local(): lax.all_gather(adapter_down_weight, 'seq', axis=0, tiled=True)  124 us
  transfers between devices with their start and end apart: 8, of which 8 were waited for; matrix products, arithmetic and copies ran while one was open for 1% of the time, Pallas kernels for 0%

commit v1 on v0

v1 whole, which is shorter than its diff:
```python
import functools

import jax
import jax.numpy as jnp
from jax import lax
from jax.experimental import pallas as pl
from jax.experimental.pallas import tpu as pltpu
from jax.sharding import PartitionSpec as P

HEAD_WIDTH = 128
LAT = 64
COLUMNS = 4
EPS = 1e-06
F32 = jnp.float32
BF16 = jnp.bfloat16
MIB = 1024 * 1024


def position(rows_z):
    seq = lax.axis_index("seq")
    y, z = seq // rows_z, seq % rows_z
    side = y // 2
    pair = jnp.where(y < 2, y, 3 - y)
    partner = (3 - y) * rows_z + z
    sibling = (y + 1 - 2 * (y % 2)) * rows_z + z
    return seq, y, z, side, pair, partner, sibling


def copy_to(src, dst, send_sem, recv_sem, target):
    return pltpu.make_async_remote_copy(
        src_ref=src,
        dst_ref=dst,
        send_sem=send_sem,
        recv_sem=recv_sem,
        device_id=target,
        device_id_type=pl.DeviceIdType.MESH,
    )


class Chain:
    def __init__(self, unit, send_sem, recv_sem, rows_z):
        self.unit, self.send_sem, self.recv_sem, self.rows_z = unit, send_sem, recv_sem, rows_z
        (self.seq, _, self.z, _, self.pair, _, self.sibling) = position(rows_z)

    def copy(self, pair, row, way, target):
        ref = self.unit(pair, row)
        return copy_to(
            ref,
            ref,
            self.send_sem.at[way * self.rows_z + row],
            self.recv_sem.at[pair * self.rows_z + row],
            {"seq": target},
        )

    def up(self, row):
        return self.copy(self.pair, row, 0, jnp.minimum(self.seq + 1, 4 * self.rows_z - 1))

    def down(self, row):
        return self.copy(self.pair, row, 1, jnp.maximum(self.seq - 1, 0))

    def across(self, row):
        return self.copy(self.pair, row, 2, self.sibling)

    def own(self):
        z = self.z

        @pl.when(z < self.rows_z - 1)
        def _():
            self.up(z).start()

        @pl.when(z > 0)
        def _():
            self.down(z).start()

        self.across(z).start()

    def step(self, t):
        z, last = self.z, self.rows_z - 1

        @pl.when(z - t >= 0)
        def _():
            row = z - t
            self.up(row).wait_recv()

            @pl.when(z < last)
            def _():
                self.up(row).start()

            self.across(row).start()

        @pl.when(z + t <= last)
        def _():
            row = z + t
            self.down(row).wait_recv()

            @pl.when(z > 0)
            def _():
                self.down(row).start()

            self.across(row).start()

    def forward(self):
        def body(t, carry):
            self.step(t)
            return carry

        lax.fori_loop(1, self.rows_z, body, 0)

    def sibling_recv(self):
        def body(row, carry):
            self.copy(1 - self.pair, row, 2, self.sibling).wait_recv()
            return carry

        lax.fori_loop(0, self.rows_z, body, 0)

    def drain(self):
        z, last = self.z, self.rows_z - 1

        def body(row, carry):
            @pl.when(jnp.logical_and(z < last, row <= z))
            def _():
                self.up(row).wait_send()

            @pl.when(jnp.logical_and(z > 0, row >= z))
            def _():
                self.down(row).wait_send()

            self.across(row).wait_send()
            return carry

        lax.fori_loop(0, self.rows_z, body, 0)


def noise_level_of(timestep_ref):
    fraction = jnp.full((1, LAT), timestep_ref[0], jnp.int32).astype(F32) / 1000.0
    return 5.0 * fraction / (1.0 + 4.0 * fraction)


def three_parts(value):
    high = value.astype(BF16)
    rest = value - high.astype(F32)
    middle = rest.astype(BF16)
    low = (rest - middle.astype(F32)).astype(BF16)
    return high, middle, low


def main_kernel(
    rows_z,
    timestep_ref,
    student_ref,
    student_gain_ref,
    student_head_ref,
    noise_ref,
    context_ref,
    patch_ref,
    gain_ref,
    query_ref,
    key_ref,
    value_ref,
    down_ref,
    up_ref,
    output_ref,
    velocity_ref,
    share_ref,
    aux_ref,
    block_ref,
    weights,
    staged,
    act_student,
    hidden,
    act,
    queries,
    kv,
    scores,
    top,
    total,
    mixed,
    w_send,
    w_recv,
    kv_send,
    kv_recv,
    swap_send,
    swap_recv,
    act_send,
    act_recv,
):
    seq, y, z, side, pair, partner, sibling = position(rows_z)
    tokens, width = student_ref.shape
    depth = query_ref.shape[0]
    groups = lax.axis_size("grp") * lax.axis_size("tp")
    group = lax.axis_index("grp") * lax.axis_size("tp") + lax.axis_index("tp")

    barrier = pltpu.get_barrier_semaphore()

    def greet(target):
        pl.semaphore_signal(
            barrier, inc=1, device_id={"seq": target}, device_id_type=pl.DeviceIdType.MESH
        )

    greet(partner)
    greet(sibling)

    @pl.when(z > 0)
    def _():
        greet(jnp.maximum(seq - 1, 0))

    @pl.when(z < rows_z - 1)
    def _():
        greet(jnp.minimum(seq + 1, 4 * rows_z - 1))

    velocity_rows = velocity_ref[pl.ds(pl.multiple_of(seq * depth, 16), depth), :]
    for which in range(2):
        head = side if which == 0 else 1 - side
        columns = pl.ds(pl.multiple_of(head * HEAD_WIDTH, HEAD_WIDTH), HEAD_WIDTH)
        folded = jnp.dot(
            output_ref[columns, :], velocity_rows, preferred_element_type=F32
        ).astype(BF16)
        rows = folded.shape[0]
        if depth > rows:
            folded = jnp.concatenate([folded, jnp.zeros((depth - rows, LAT), BF16)], axis=0)
        last = jnp.concatenate([down_ref[...], folded], axis=1)
        slot = weights.at[2 * pair + side, z] if which == 0 else staged
        slot[:, 0:128] = query_ref[:, columns]
        slot[:, 128:256] = key_ref[:, columns]
        slot[:, 256:384] = value_ref[:, columns]
        slot[:, 384:512] = last

    @pl.when(jnp.logical_and(z > 0, z < rows_z - 1))
    def _():
        pl.semaphore_wait(barrier, 4)

    @pl.when(jnp.logical_or(z == 0, z == rows_z - 1))
    def _():
        pl.semaphore_wait(barrier, 3)

    swap = copy_to(
        staged, weights.at[2 * pair + side, z], swap_send, swap_recv, {"seq": partner}
    )
    swap.start()

    chunk = 16

    def student_rows(i, carry):
        rows = pl.ds(pl.multiple_of(i * chunk, chunk), chunk)
        value = student_ref[rows, :].astype(F32)
        scale = lax.rsqrt(jnp.mean(value * value, axis=-1, keepdims=True) + EPS)
        act_student[rows, :] = (value * scale * student_gain_ref[...]).astype(BF16)
        return carry

    lax.fori_loop(0, tokens // chunk, student_rows, 0)

    copy_to(
        staged, weights.at[2 * pair + 1 - side, z], swap_send, swap_recv, {"seq": partner}
    ).wait_recv()
    w_chain = Chain(lambda p, r: weights.at[pl.ds(2 * p, 2), r], w_send, w_recv, rows_z)
    w_chain.own()

    level = noise_level_of(timestep_ref)
    latent = jnp.dot(act_student[...], student_head_ref[...], preferred_element_type=F32)
    noisy = ((1.0 - level) * latent + level * noise_ref[...].astype(F32)).astype(BF16)
    slab = 512 if width % 512 == 0 else width

    def hidden_columns(i, carry):
        columns = pl.ds(pl.multiple_of(i * slab, slab), slab)
        hidden[:, columns] = jnp.dot(
            noisy, patch_ref[:, columns], preferred_element_type=F32
        ) + context_ref[:, columns].astype(F32)
        return carry

    lax.fori_loop(0, width // slab, hidden_columns, 0)

    def act_rows(i, carry):
        value = hidden[pl.ds(pl.multiple_of(i * chunk, chunk), chunk), :]
        scale = lax.rsqrt(jnp.mean(value * value, axis=-1, keepdims=True) + EPS)
        act[side, pl.ds(pl.multiple_of(i * chunk, chunk), chunk), :] = (
            value * scale * gain_ref[...]
        ).astype(BF16)
        return carry

    lax.fori_loop(0, tokens // chunk, act_rows, 0)
    act_copy = copy_to(act.at[side], act.at[side], act_send, act_recv, {"seq": partner})
    act_copy.start()

    mine = pl.ds(pl.multiple_of(group * 8, 8), 8)
    queries[0, 0:tokens, 0:LAT] = latent
    queries[1, 0:tokens, 0:LAT] = noisy.astype(F32)
    parts = three_parts(hidden[mine, :])
    residual = sum(
        jnp.dot(part, velocity_ref[...], preferred_element_type=F32) for part in parts
    )
    aux_ref[0:8, :] = residual
    aux_ref[8:16, :] = queries[0, mine, 0:LAT]
    aux_ref[16:24, :] = queries[1, mine, 0:LAT]
    grad_rows = width // groups
    start = group * grad_rows
    if grad_rows % 128:
        start = start - (group % 2) * LAT
    block_ref[...] = act_student[
        :, pl.ds(pl.multiple_of(start, 128), block_ref.shape[1])
    ]

    w_chain.forward()
    w_chain.sibling_recv()
    copy_to(
        act.at[1 - side], act.at[1 - side], act_send, act_recv, {"seq": partner}
    ).wait_recv()

    both = jnp.concatenate([act[0], act[1]], axis=0)
    span = width // COLUMNS
    product = None
    for place, column in enumerate((0, 3, 1, 2)):
        term = jnp.dot(
            both[:, column * span : (column + 1) * span],
            weights[place].reshape(span, 512),
            preferred_element_type=F32,
        )
        product = term if product is None else product + term

    def fold_rows(r, carry):
        for place in range(COLUMNS):
            carry = carry + weights[place, r, 0 : min(depth, HEAD_WIDTH), 384:512].astype(F32)
        return carry

    folded = lax.fori_loop(
        0, rows_z, fold_rows, jnp.zeros((min(depth, HEAD_WIDTH), 128), F32)
    )[:, LAT:]
    high = folded.astype(BF16)
    low_part = (folded - high.astype(F32)).astype(BF16)
    values = product[:, 256:384].astype(BF16)
    moved = jnp.dot(
        values, jnp.concatenate([high, low_part], axis=1), preferred_element_type=F32
    )
    moved = (moved[:, :LAT] + moved[:, LAT:]).astype(BF16)
    kv[pair, z, 0 : 2 * tokens, :] = product[:, 128:256].astype(BF16)
    kv[pair, z, 2 * tokens : 3 * tokens, :] = jnp.concatenate(
        [moved[:tokens], moved[tokens:]], axis=1
    )
    kv_chain = Chain(lambda p, r: kv.at[p, r], kv_send, kv_recv, rows_z)
    kv_chain.own()

    low = product[:, 384 : 384 + LAT].astype(BF16)
    head_columns = pl.ds(pl.multiple_of(side * HEAD_WIDTH, HEAD_WIDTH), HEAD_WIDTH)
    plain = product[:, 0:128]
    queries[0] = plain
    queries[1] = plain + jnp.dot(low, up_ref[:, head_columns], preferred_element_type=F32)
    asked = jnp.concatenate([queries[0], queries[1]], axis=0).astype(BF16)

    kv_chain.forward()
    kv_chain.sibling_recv()

    top[...] = jnp.full(top.shape, -1e30, F32)
    factor = HEAD_WIDTH**-0.5

    def score_unit(u, carry):
        keys = kv[u // rows_z, u % rows_z, 0 : 2 * tokens, :]
        found = (
            lax.dot_general(asked, keys, (((1,), (1,)), ((), ())), preferred_element_type=F32)
            * factor
        )
        scores[u] = found
        top[...] = jnp.maximum(
            top[...], jnp.maximum(found[:, :tokens], found[:, tokens:])
        )
        return carry

    lax.fori_loop(0, 2 * rows_z, score_unit, 0)
    peak = jnp.max(top[...], axis=-1, keepdims=True)
    top[...] = jnp.broadcast_to(peak, top.shape)
    total[...] = jnp.zeros(total.shape, F32)
    mixed[...] = jnp.zeros(mixed.shape, F32)

    def mix_unit(u, carry):
        shift = top[...]
        left = jnp.exp(scores[u, :, 0:tokens] - shift)
        right = jnp.exp(scores[u, :, tokens : 2 * tokens] - shift)
        total[...] += left + right
        packed = kv[u // rows_z, u % rows_z, 2 * tokens : 3 * tokens, :]
        stacked = jnp.concatenate([packed[:, :LAT], packed[:, LAT:]], axis=0)
        mixed[...] += jnp.dot(
            jnp.concatenate([left, right], axis=1).astype(BF16),
            stacked,
            preferred_element_type=F32,
        )
        return carry

    lax.fori_loop(0, 2 * rows_z, mix_unit, 0)
    attended = mixed[...] / jnp.sum(total[...], axis=-1, keepdims=True)
    share_ref[...] = jnp.concatenate(
        [attended[: 2 * tokens], attended[2 * tokens :]], axis=1
    )

    swap.wait_send()
    act_copy.wait_send()
    w_chain.drain()
    kv_chain.drain()


def tail_kernel(
    rows_z,
    timestep_ref,
    share_ref,
    aux_ref,
    block_ref,
    diff_ref,
    grad_ref,
    met,
    tiles,
    window,
    outgoing,
    arrived,
    pieces,
    send1,
    recv1,
    send2,
    recv2,
    send3,
    recv3,
    send4,
    recv4,
):
    seq, y, z, side, pair, partner, sibling = position(rows_z)
    tp_size = lax.axis_size("tp")
    groups = lax.axis_size("grp") * tp_size
    group = lax.axis_index("grp") * tp_size + lax.axis_index("tp")
    seqs = 4 * rows_z
    tokens = 8 * groups
    grad_rows = grad_ref.shape[0]
    owners = grad_rows // 16
    me = side * groups + group

    def member(j):
        other = j // groups
        column = jnp.where(other == 0, pair, 3 - pair)
        g = j % groups
        return {"grp": g // tp_size, "seq": column * rows_z + z, "tp": g % tp_size}

    def peer(g):
        return {"grp": g // tp_size, "tp": g % tp_size}

    def each(count, skip, act):
        def body(j, carry):
            @pl.when(j != skip)
            def _():
                act(j)

            return carry

        lax.fori_loop(0, count, body, 0)

    barrier = pltpu.get_barrier_semaphore()

    def greet(target):
        pl.semaphore_signal(
            barrier, inc=1, device_id=target, device_id_type=pl.DeviceIdType.MESH
        )

    each(2 * groups, me, lambda j: greet(member(j)))

    def greet_seq(p):
        @pl.when(p != partner)
        def _():
            greet({"seq": p})

    each(seqs, seq, greet_seq)
    pl.semaphore_wait(barrier, 2 * groups - 1 + seqs - 2)

    def rows_of(j):
        return share_ref.at[pl.ds(pl.multiple_of(j * 8, 8), 8), :]

    each(
        2 * groups,
        me,
        lambda j: copy_to(
            rows_of(j), met.at[me], send1.at[j], recv1.at[me], member(j)
        ).start(),
    )
    met[me] = share_ref[pl.ds(pl.multiple_of(me * 8, 8), 8), :]
    each(
        2 * groups,
        me,
        lambda j: copy_to(
            rows_of(j), met.at[j], send1.at[j], recv1.at[j], member(j)
        ).wait_recv(),
    )
    shares = jnp.sum(met[...], axis=0)
    level = noise_level_of(timestep_ref)
    residual, latent, noisy = aux_ref[0:8, :], aux_ref[8:16, :], aux_ref[16:24, :]
    real = noisy - level * (residual + shares[:, :LAT])
    fake = noisy - level * (residual + shares[:, LAT:])
    tiles[group] = jnp.concatenate([fake - real, jnp.abs(latent - real)], axis=1)
    each(
        groups,
        group,
        lambda g: copy_to(
            tiles.at[group], tiles.at[group], send2.at[g], recv2.at[group], peer(g)
        ).start(),
    )
    each(
        groups,
        group,
        lambda g: copy_to(
            tiles.at[g], tiles.at[g], send2.at[g], recv2.at[g], peer(g)
        ).wait_recv(),
    )
    all_tiles = tiles[...]
    gap = jnp.sum(all_tiles, axis=0)
    lane = lax.broadcasted_iota(jnp.int32, gap.shape, 1)
    gap = jnp.where(lane >= LAT, gap, 0.0)
    diff = all_tiles.reshape(tokens, 128)[:, :LAT]
    split = jnp.concatenate(three_parts(diff), axis=1)
    found = lax.dot_general(
        block_ref[...], split, (((0,), (0,)), ((), ())), preferred_element_type=F32
    )
    window[...] = found[:, :LAT] + found[:, LAT : 2 * LAT] + found[:, 2 * LAT :]
    offset = (group % 2) * LAT if grad_rows % 128 else 0

    def fill(p, carry):
        first = window[pl.ds(pl.multiple_of(offset + p * 8, 8), 8), :]
        second = window[pl.ds(pl.multiple_of(offset + grad_rows // 2 + p * 8, 8), 8), :]
        outgoing[p, 0:8, :] = jnp.concatenate([first, second], axis=1)
        outgoing[p, 8:16, :] = gap
        return carry

    lax.fori_loop(0, owners, fill, 0)

    def fill_rest(p, carry):
        outgoing[p, 0:8, :] = jnp.zeros((8, 128), F32)
        outgoing[p, 8:16, :] = gap
        return carry

    lax.fori_loop(owners, seqs, fill_rest, 0)
    each(
        seqs,
        seq,
        lambda p: copy_to(
            outgoing.at[p], arrived.at[seq], send3.at[p], recv3.at[seq], {"seq": p}
        ).start(),
    )
    arrived[seq] = outgoing[seq]
    each(
        seqs,
        seq,
        lambda p: copy_to(
            outgoing.at[p], arrived.at[p], send3.at[p], recv3.at[p], {"seq": p}
        ).wait_recv(),
    )
    sums = jnp.sum(arrived[...], axis=0)
    gap_total = jnp.sum(sums[8:16, :], keepdims=True)
    count = tokens * seqs * LAT
    scale = 1.0 / (gap_total / count + 1e-05)
    diff_ref[...] = scale * diff
    token_scale = float(tokens * seqs) ** -0.5

    @pl.when(seq < owners)
    def _():
        pieces[seq] = (scale * token_scale) * sums[0:8, :]
        each(
            seqs,
            seq,
            lambda p: copy_to(
                pieces.at[seq], pieces.at[seq], send4.at[p], recv4.at[seq], {"seq": p}
            ).start(),
        )

    each(
        owners,
        seq,
        lambda p: copy_to(
            pieces.at[p], pieces.at[p], send4.at[p], recv4.at[p], {"seq": p}
        ).wait_recv(),
    )
    whole = pieces[...].reshape(grad_rows // 2, 128)
    grad_ref[0 : grad_rows // 2, :] = whole[:, :LAT]
    grad_ref[grad_rows // 2 :, :] = whole[:, LAT:]

    each(
        2 * groups,
        me,
        lambda j: copy_to(
            rows_of(j), met.at[me], send1.at[j], recv1.at[me], member(j)
        ).wait_send(),
    )
    each(
        groups,
        group,
        lambda g: copy_to(
            tiles.at[group], tiles.at[group], send2.at[g], recv2.at[group], peer(g)
        ).wait_send(),
    )
    each(
        seqs,
        seq,
        lambda p: copy_to(
            outgoing.at[p], arrived.at[seq], send3.at[p], recv3.at[seq], {"seq": p}
        ).wait_send(),
    )

    @pl.when(seq < owners)
    def _():
        each(
            seqs,
            seq,
            lambda p: copy_to(
                pieces.at[seq], pieces.at[seq], send4.at[p], recv4.at[seq], {"seq": p}
            ).wait_send(),
        )


def local(
    student_hidden_states,
    student_norm_gain,
    student_output_head,
    noise,
    timestep,
    context,
    patch_embedding_input,
    attention_norm_gain,
    query_weight,
    key_weight,
    value_weight,
    adapter_down_weight,
    adapter_up_weight,
    output_weight,
    velocity_head_output,
):
    tokens, width = student_hidden_states.shape
    depth = query_weight.shape[0]
    seqs = lax.axis_size("seq")
    rows_z = seqs // COLUMNS
    groups = lax.axis_size("grp") * lax.axis_size("tp")
    grad_rows = width // groups
    window = grad_rows + LAT if grad_rows % 128 else grad_rows
    vmem = pl.BlockSpec(memory_space=pltpu.VMEM)
    smem = pl.BlockSpec(memory_space=pltpu.SMEM)
    dma = pltpu.SemaphoreType.DMA
    share, aux, block = pl.pallas_call(
        functools.partial(main_kernel, rows_z),
        out_shape=(
            jax.ShapeDtypeStruct((2 * tokens, 2 * LAT), F32),
            jax.ShapeDtypeStruct((24, LAT), F32),
            jax.ShapeDtypeStruct((tokens, window), BF16),
        ),
        in_specs=[smem] + [vmem] * 14,
        out_specs=(vmem, vmem, vmem),
        scratch_shapes=[
            pltpu.VMEM((COLUMNS, rows_z, depth, 512), BF16),
            pltpu.VMEM((depth, 512), BF16),
            pltpu.VMEM((tokens, width), BF16),
            pltpu.VMEM((tokens, width), F32),
            pltpu.VMEM((2, tokens, width), BF16),
            pltpu.VMEM((2, 2 * tokens, HEAD_WIDTH), F32),
            pltpu.VMEM((2, rows_z, 3 * tokens, 128), BF16),
            pltpu.VMEM((2 * rows_z, 4 * tokens, 2 * tokens), F32),
            pltpu.VMEM((4 * tokens, tokens), F32),
            pltpu.VMEM((4 * tokens, tokens), F32),
            pltpu.VMEM((4 * tokens, LAT), F32),
            dma((3 * rows_z,)),
            dma((2 * rows_z,)),
            dma((3 * rows_z,)),
            dma((2 * rows_z,)),
            dma,
            dma,
            dma,
            dma,
        ],
        compiler_params=pltpu.CompilerParams(
            collective_id=0, has_side_effects=True, vmem_limit_bytes=52 * MIB
        ),
    )(
        timestep,
        student_hidden_states,
        student_norm_gain.reshape(1, width),
        student_output_head,
        noise,
        context,
        patch_embedding_input,
        attention_norm_gain.reshape(1, width),
        query_weight,
        key_weight,
        value_weight,
        adapter_down_weight,
        adapter_up_weight,
        output_weight,
        velocity_head_output,
    )
    return pl.pallas_call(
        functools.partial(tail_kernel, rows_z),
        out_shape=(
            jax.ShapeDtypeStruct((tokens, LAT), F32),
            jax.ShapeDtypeStruct((grad_rows, LAT), F32),
        ),
        in_specs=[smem] + [vmem] * 3,
        out_specs=(vmem, vmem),
        scratch_shapes=[
            pltpu.VMEM((2 * groups, 8, 128), F32),
            pltpu.VMEM((groups, 8, 128), F32),
            pltpu.VMEM((window, LAT), F32),
            pltpu.VMEM((seqs, 16, 128), F32),
            pltpu.VMEM((seqs, 16, 128), F32),
            pltpu.VMEM((grad_rows // 16, 8, 128), F32),
            dma((2 * groups,)),
            dma((2 * groups,)),
            dma((groups,)),
            dma((groups,)),
            dma((seqs,)),
            dma((seqs,)),
            dma((seqs,)),
            dma((grad_rows // 16,)),
        ],
        compiler_params=pltpu.CompilerParams(
            collective_id=1, has_side_effects=True, vmem_limit_bytes=32 * MIB
        ),
    )(timestep, share, aux, block)


def solution(mesh):
    heads = P("seq", ("grp", "tp"))
    in_specs = (
        P("seq", None),
        P(),
        P(),
        P("seq", None),
        P(),
        P("seq", None),
        P(),
        P(),
        heads,
        heads,
        heads,
        P("seq", None),
        P(None, ("grp", "tp")),
        P(("grp", "tp"), "seq"),
        P(),
    )
    out_specs = (P("seq", None), P(("grp", "tp"), None))
    return jax.shard_map(local, mesh=mesh, in_specs=in_specs, out_specs=out_specs, check_vma=False)
```

time: 2180 us -> 180 us (0.08)
  waiting for transfers between devices: 1870 us -> 0 us
  blocking collectives: 238 us -> 0 us
  Pallas kernels: 0 us -> 171 us
  matrix products: 25.2 us -> 0 us
    all_gather x6 -> x0, waiting for transfers between devices: 1210 us -> none  [the longest x1 228 us: local(): lax.all_gather(value_weight, 'seq', axis=0, tiled=True)]
    psum x2 -> x0, waiting for transfers between devices: 659 us -> none  [the longest x1 399 us: local(): grad_total, gap_total = lax.psum((grad_part, gap_part), 'seq')]
    pallas_call x0 -> x2, Pallas kernels: none -> 171 us  [the longest x1 119 us: local(): pl.pallas_call(functools.partial(main_kernel, rows_z), out_shape=(jax.Sha...]
    all_gather x1 -> x0, blocking collectives: 124 us -> none  [local(): lax.all_gather(adapter_down_weight, 'seq', axis=0, tiled=True)]
    psum x1 -> x0, blocking collectives: 113 us -> none  [local(): grad_total, gap_total = lax.psum((grad_part, gap_part), 'seq')]
    dot_general x12 -> x0, matrix products: 25.2 us -> none  [the longest x3 8 us: local(): jnp.dot(activation, block, preferred_element_type=jnp.float32)]
  transfers between devices with their start and end apart: 8 -> 0, of which waited for: 8 -> 0; matrix products, arithmetic and copies ran while one was open for 1% -> 0% of each run, Pallas kernels for 0% -> 0%
where the time goes in v1:
time: 180 us
  Pallas kernels  171 us (95%)
  local copies, waits for them, and re-layouts  7.93 us (4%)
    pallas_call x1, Pallas kernels, local(): pl.pallas_call(functools.partial(main_kernel, rows_z), out_shape=(jax.Sha...  119 us
    pallas_call x1, Pallas kernels, local(): pl.pallas_call(functools.partial(tail_kernel, rows_z), out_shape=(jax.Sha...  51.9 us
    unnamed x21, local copies, waits for them, and re-layouts  6.48 us

profile of v1, /device:TPU:24, one launch (start us, length us, event | category | flops | bytes accessed | tf_op | source)
XLA Modules:
  0.0 180.0 jit_solution(3609064283554891924)
XLA Ops:
  0.6 0.0 copy-start.7
  1.4 0.8 copy.18.noise_ref
  2.2 0.9 copy.19.down_ref
  3.1 1.0 copy.20.output_ref
  4.1 2.3 %copy.17.student_head_ref = bf16[5120,64]{1,0:T(8,128)(2,1)} copy(bf16[5120,64]{0,1:T(8,128)(2,1)} %param.17) | data formatting | bytes 1310720 | tf_op args[2]
  6.4 0.0 copy-done.7
  6.4 0.0 copy-start
  6.4 0.0 copy-start.1
  6.4 0.0 copy-start.2
  6.4 0.0 copy-start.3
  6.4 0.0 copy-start.4
  6.4 0.0 copy-start.5
  6.4 0.0 copy-start.6
  6.5 1.4 copy.21.velocity_ref
  7.9 0.0 copy-done
  7.9 0.0 copy-done.1
  7.9 0.0 copy-done.2
  7.9 0.0 copy-done.3
  7.9 0.0 copy-done.4
  7.9 0.0 copy-done.5
  7.9 0.0 copy-done.6
  7.9 118.7 %shard_map.158 = (f32[256,128]{1,0:T(8,128)S(1)}, f32[24,64]{1,0:T(8,128)S(1)}, bf16[128,384]{1,0:T(8,128)(2,1)S(1)}) custom-call(s32[1]{0:T(128)S(6)} %copy.24.timestep_ref, bf16[128,5120]{1,0:T(8,128)(2,1)} %student_ref.1, f32[1,5120]{1,0:T(1,128)S(1)} %bitcast.2, bf16[5120,64]{1,0:T(8,128)(2,1)} %copy.17.student_head_ref, ...), custom_call_target="tpu_custom_call" | custom-call | tf_op jit(solution)/shard_map/pallas_call | solution.py:636
  126.6 51.9 %shard_map.159 = (f32[128,64]{1,0:T(8,128)S(1)}, f32[320,64]{1,0:T(8,128)S(1)}) custom-call(s32[1]{0:T(128)S(6)} %copy.24.timestep_ref, f32[256,128]{1,0:T(8,128)S(1)} %get-tuple-element.5.share_ref, f32[24,64]{1,0:T(8,128)S(1)} %get-tuple-element.6.aux_ref, bf16[128,384]{1,0:T(8,128)(2,1)S(1)} %get-tuple-element.7.block_ref), custom_call_target="tpu_custom_call" | custom-call | tf_op jit(solution)/shard_map/pallas_call | solution.py:686
  178.5 0.7 copy.22
  179.2 0.8 copy.23
Async XLA Ops:
  0.6 5.8 %copy-start.7 = (bf16[5120,64]{0,1:T(8,128)(2,1)S(1)}, bf16[5120,64]{0,1:T(8,128)(2,1)}, u32[]{:S(2)}) copy-start(bf16[5120,64]{0,1:T(8,128)(2,1)} %param.29) | copy-start | bytes 1966084
  6.4 1.5 copy-start
  6.4 1.5 copy-start.1
  6.4 1.5 copy-start.2
  6.4 1.5 copy-start.3
  6.4 1.5 copy-start.4
  6.4 1.5 copy-start.5
  6.4 1.5 copy-start.6

commit v2 on v0

v2 whole, which is shorter than its diff:
```python
import functools

import jax
import jax.numpy as jnp
from jax import lax
from jax.experimental import pallas as pl
from jax.experimental.pallas import tpu as pltpu
from jax.sharding import PartitionSpec as P

HEAD_WIDTH = 128
LAT = 64
COLUMNS = 4
EPS = 1e-06
F32 = jnp.float32
BF16 = jnp.bfloat16
MIB = 1024 * 1024


def position(rows_z):
    seq = lax.axis_index("seq")
    y, z = seq // rows_z, seq % rows_z
    side = y // 2
    pair = jnp.where(y < 2, y, 3 - y)
    partner = (3 - y) * rows_z + z
    sibling = (y + 1 - 2 * (y % 2)) * rows_z + z
    return seq, y, z, side, pair, partner, sibling


def copy_to(src, dst, send_sem, recv_sem, target):
    return pltpu.make_async_remote_copy(
        src_ref=src,
        dst_ref=dst,
        send_sem=send_sem,
        recv_sem=recv_sem,
        device_id=target,
        device_id_type=pl.DeviceIdType.MESH,
    )


class Chain:
    def __init__(self, unit, send_sem, recv_sem, rows_z):
        self.unit, self.send_sem, self.recv_sem, self.rows_z = unit, send_sem, recv_sem, rows_z
        (self.seq, _, self.z, _, self.pair, _, self.sibling) = position(rows_z)

    def copy(self, pair, row, way, target):
        ref = self.unit(pair, row)
        return copy_to(
            ref,
            ref,
            self.send_sem.at[way * self.rows_z + row],
            self.recv_sem.at[pair * self.rows_z + row],
            {"seq": target},
        )

    def up(self, row):
        return self.copy(self.pair, row, 0, jnp.minimum(self.seq + 1, 4 * self.rows_z - 1))

    def down(self, row):
        return self.copy(self.pair, row, 1, jnp.maximum(self.seq - 1, 0))

    def across(self, row):
        return self.copy(self.pair, row, 2, self.sibling)

    def own(self):
        z = self.z

        @pl.when(z < self.rows_z - 1)
        def _():
            self.up(z).start()

        @pl.when(z > 0)
        def _():
            self.down(z).start()

        self.across(z).start()

    def step(self, t):
        z, last = self.z, self.rows_z - 1

        @pl.when(z - t >= 0)
        def _():
            row = z - t
            self.up(row).wait_recv()

            @pl.when(z < last)
            def _():
                self.up(row).start()

            self.across(row).start()

        @pl.when(z + t <= last)
        def _():
            row = z + t
            self.down(row).wait_recv()

            @pl.when(z > 0)
            def _():
                self.down(row).start()

            self.across(row).start()

    def forward(self):
        def body(t, carry):
            self.step(t)
            return carry

        lax.fori_loop(1, self.rows_z, body, 0)

    def sibling_recv(self):
        def body(row, carry):
            self.copy(1 - self.pair, row, 2, self.sibling).wait_recv()
            return carry

        lax.fori_loop(0, self.rows_z, body, 0)

    def drain(self):
        z, last = self.z, self.rows_z - 1

        def body(row, carry):
            @pl.when(jnp.logical_and(z < last, row <= z))
            def _():
                self.up(row).wait_send()

            @pl.when(jnp.logical_and(z > 0, row >= z))
            def _():
                self.down(row).wait_send()

            self.across(row).wait_send()
            return carry

        lax.fori_loop(0, self.rows_z, body, 0)


def noise_level_of(timestep_ref):
    fraction = jnp.full((1, LAT), timestep_ref[0], jnp.int32).astype(F32) / 1000.0
    return 5.0 * fraction / (1.0 + 4.0 * fraction)


def three_parts(value):
    high = value.astype(BF16)
    rest = value - high.astype(F32)
    middle = rest.astype(BF16)
    low = (rest - middle.astype(F32)).astype(BF16)
    return high, middle, low


def kernel(
    rows_z,
    timestep_ref,
    student_ref,
    student_gain_ref,
    student_head_ref,
    noise_ref,
    context_ref,
    patch_ref,
    gain_ref,
    query_ref,
    key_ref,
    value_ref,
    down_ref,
    up_ref,
    output_ref,
    velocity_ref,
    diff_ref,
    grad_ref,
    qk_weights,
    dv_weights,
    qk_staged,
    vd_staged,
    vd_mail,
    placed,
    fold_out,
    fold_column,
    fold_rows,
    fold_arrived,
    fold_whole,
    act_student,
    hidden,
    act,
    latents,
    first,
    second,
    keys,
    values,
    scores,
    top,
    total,
    mixed,
    share,
    met,
    halves,
    tiles,
    window,
    y_out,
    y_in,
    z_out,
    z_in,
    pieces,
    columns,
    qk_send,
    qk_recv,
    dv_send,
    dv_recv,
    k_send,
    k_recv,
    v_send,
    v_recv,
    one_send,
    one_recv,
):
    seq, y, z, side, pair, partner, sibling = position(rows_z)
    tokens, width = student_ref.shape
    depth = query_ref.shape[0]
    tp_size = lax.axis_size("tp")
    tp = lax.axis_index("tp")
    grp = lax.axis_index("grp")
    groups = lax.axis_size("grp") * tp_size
    group = grp * tp_size + tp
    z_hi, core = grp // 2, grp % 2
    ranks = 2 * tp_size
    rank = core * tp_size + tp
    members = 2 * ranks
    me = side * ranks + rank
    span = width // COLUMNS
    seqs = COLUMNS * rows_z
    here = {"seq": partner}

    def member(k):
        j = (me + k) % members
        column = jnp.where(j // ranks == 0, pair, 3 - pair)
        r = j % ranks
        return j, {
            "grp": z_hi * 2 + r // tp_size,
            "seq": column * rows_z + z,
            "tp": r % tp_size,
        }

    def fellow(k):
        r = (rank + k) % ranks
        return {"grp": z_hi * 2 + r // tp_size, "tp": r % tp_size}

    def in_column(k):
        other = (z + k) % rows_z
        return other, {"seq": y * rows_z + other}

    def in_row(k):
        other = (y + k) % COLUMNS
        return other, {"seq": other * rows_z + z}

    def joined(ref, sem, count):
        part = ref.at[pl.ds(0, count)]
        return copy_to(part, part, one_send.at[sem], one_recv.at[sem], here)

    def send(src, dst, sem, target):
        copy_to(src, dst, one_send.at[sem], one_recv.at[sem], target).start()

    barrier = pltpu.get_barrier_semaphore()

    def greet(target):
        pl.semaphore_signal(
            barrier, inc=1, device_id=target, device_id_type=pl.DeviceIdType.MESH
        )

    for k in range(1, COLUMNS):
        greet(in_row(k)[1])
    for k in range(1, rows_z):
        greet(in_column(k)[1])
    for k in range(1, members):
        if k != ranks:
            greet(member(k)[1])
    greet({"grp": (1 - z_hi) * 2 + core})

    wide = placed.shape[0]
    begin = seq * depth
    offset = begin % 128
    placed[...] = jnp.zeros(placed.shape, BF16)
    placed[pl.ds(pl.multiple_of(offset, 32), depth), :] = output_ref[...]
    folded = jnp.dot(
        velocity_ref[:, pl.ds(pl.multiple_of(begin - offset, 128), wide)],
        placed[...],
        preferred_element_type=F32,
    )
    fold_out[0] = folded[:, :HEAD_WIDTH]
    fold_out[1] = folded[:, HEAD_WIDTH:]
    fold_column[y] = fold_out[side]
    down = down_ref[...].astype(F32).T.astype(BF16)
    own_columns = pl.ds(pl.multiple_of(side * HEAD_WIDTH, HEAD_WIDTH), HEAD_WIDTH)
    other_columns = pl.ds(pl.multiple_of((1 - side) * HEAD_WIDTH, HEAD_WIDTH), HEAD_WIDTH)
    mine = 2 * pair + side
    theirs = 2 * pair + 1 - side
    qk_weights[mine, z, :, 0:128] = query_ref[:, own_columns]
    qk_weights[mine, z, :, 128:256] = key_ref[:, own_columns]
    qk_staged[:, 0:128] = query_ref[:, other_columns]
    qk_staged[:, 128:256] = key_ref[:, other_columns]
    vd_staged[:, 0:128] = value_ref[:, other_columns]
    vd_staged[:, 128:256] = jnp.concatenate([down, down], axis=1)

    pl.semaphore_wait(barrier, 1 + COLUMNS - 1 + rows_z - 1 + members - 2)

    send(qk_staged, qk_weights.at[mine, z], 0, here)
    send(vd_staged, vd_mail, 1, here)
    for k in range(1, COLUMNS):
        other, target = in_row(k)
        send(fold_out.at[other // 2], fold_column.at[y], 2, target)

    chunk = 16

    def student_rows(i, carry):
        rows = pl.ds(pl.multiple_of(i * chunk, chunk), chunk)
        value = student_ref[rows, :].astype(F32)
        scale = lax.rsqrt(jnp.mean(value * value, axis=-1, keepdims=True) + EPS)
        act_student[rows, :] = (value * scale * student_gain_ref[...]).astype(BF16)
        return carry

    lax.fori_loop(0, tokens // chunk, student_rows, 0)

    copy_to(
        qk_staged, qk_weights.at[theirs, z], one_send.at[0], one_recv.at[0], here
    ).wait_recv()
    qk = Chain(lambda p, r: qk_weights.at[pl.ds(2 * p, 2), r], qk_send, qk_recv, rows_z)
    dv = Chain(lambda p, r: dv_weights.at[pl.ds(2 * p, 2), r], dv_send, dv_recv, rows_z)
    qk.own()

    joined(fold_column, 2, COLUMNS - 1).wait_recv()
    fold_rows[...] = jnp.sum(fold_column[...], axis=0).reshape(fold_rows.shape)
    fold_arrived[z] = fold_rows[z]
    for k in range(1, rows_z):
        other, target = in_column(k)
        send(fold_rows.at[other], fold_arrived.at[z], 3, target)

    level = noise_level_of(timestep_ref)
    latent = lax.dot_general(
        act_student[...],
        student_head_ref[...],
        (((1,), (1,)), ((), ())),
        preferred_element_type=F32,
    )
    noise = noise_ref[...].astype(F32).T
    noisy = ((1.0 - level) * latent + level * noise).astype(BF16)
    slab = 512 if width % 512 == 0 else width

    def hidden_columns(i, carry):
        part = pl.ds(pl.multiple_of(i * slab, slab), slab)
        hidden[:, part] = jnp.dot(
            noisy, patch_ref[:, part], preferred_element_type=F32
        ) + context_ref[:, part].astype(F32)
        return carry

    lax.fori_loop(0, width // slab, hidden_columns, 0)

    joined(fold_arrived, 3, rows_z - 1).wait_recv()
    fold_whole[z] = jnp.sum(fold_arrived[...], axis=0)
    for k in range(1, rows_z):
        other, target = in_column(k)
        send(fold_whole.at[z], fold_whole.at[z], 4, target)
    qk.step(1)

    def act_rows(i, carry):
        rows = pl.ds(pl.multiple_of(i * chunk, chunk), chunk)
        value = hidden[rows, :]
        scale = lax.rsqrt(jnp.mean(value * value, axis=-1, keepdims=True) + EPS)
        act[side, rows, :] = (value * scale * gain_ref[...]).astype(BF16)
        return carry

    lax.fori_loop(0, tokens // chunk, act_rows, 0)
    send(act.at[side], act.at[side], 5, here)

    joined(fold_whole, 4, rows_z - 1).wait_recv()
    whole = fold_whole[...].reshape(LAT, HEAD_WIDTH)
    high = whole.astype(BF16)
    rest = (whole - high.astype(F32)).astype(BF16)
    split = jnp.concatenate([high, rest], axis=0)
    copy_to(vd_staged, vd_mail, one_send.at[1], one_recv.at[1], here).wait_recv()
    for place, value, lower in (
        (mine, value_ref[:, own_columns], down),
        (theirs, vd_mail[:, 0:128], vd_mail[:, 128 : 128 + LAT]),
    ):
        moved = lax.dot_general(
            value, split, (((1,), (1,)), ((), ())), preferred_element_type=F32
        )
        moved = (moved[:, :LAT] + moved[:, LAT:]).astype(BF16)
        dv_weights[place, z] = jnp.concatenate([lower, moved], axis=1)
    dv.own()
    qk.step(2)

    taken = pl.ds(pl.multiple_of(rank * 16, 16), 16)
    latents[0] = latent
    latents[1] = noisy.astype(F32)
    parts = jnp.concatenate(three_parts(hidden[taken, :]), axis=0)
    residual = lax.dot_general(
        parts, velocity_ref[...], (((1,), (1,)), ((), ())), preferred_element_type=F32
    )
    residual = residual[0:16] + residual[16:32] + residual[32:48]

    def both_steps(t, carry):
        dv.step(t)
        qk.step(t + 2)
        return carry

    lax.fori_loop(1, rows_z, both_steps, 0)
    copy_to(
        act.at[1 - side], act.at[1 - side], one_send.at[5], one_recv.at[5], here
    ).wait_recv()

    def project(place, column, fresh):
        part = pl.ds(pl.multiple_of(column * span, span), span)
        rows = act[:, :, part].reshape(2 * tokens, span)
        one = jnp.dot(
            rows, qk_weights[place].reshape(span, 256), preferred_element_type=F32
        )
        two = jnp.dot(
            rows, dv_weights[place].reshape(span, 128), preferred_element_type=F32
        )
        first[...] = one if fresh else first[...] + one
        second[...] = two if fresh else second[...] + two

    project(2 * pair, pair, True)
    project(2 * pair + 1, 3 - pair, False)
    qk.sibling_recv()
    dv.sibling_recv()
    project(2 - 2 * pair, 1 - pair, False)
    project(3 - 2 * pair, 2 + pair, False)

    keys[pair, z] = first[:, 128:256].astype(BF16)
    k_chain = Chain(lambda p, r: keys.at[p, r], k_send, k_recv, rows_z)
    v_chain = Chain(lambda p, r: values.at[p, r], v_send, v_recv, rows_z)
    k_chain.own()
    moved = second[:, LAT:].astype(BF16)
    values[pair, z] = jnp.concatenate([moved[:tokens], moved[tokens:]], axis=1)
    v_chain.own()

    low = second[:, :LAT].astype(BF16)
    plain = first[:, 0:128]
    fake = plain + jnp.dot(low, up_ref[:, own_columns], preferred_element_type=F32)
    asked = jnp.concatenate([plain, fake], axis=0).astype(BF16)
    top[...] = jnp.full(top.shape, -1e30, F32)
    factor = HEAD_WIDTH**-0.5

    def score_unit(p, r):
        found = (
            lax.dot_general(
                asked, keys[p, r], (((1,), (1,)), ((), ())), preferred_element_type=F32
            )
            * factor
        )
        scores[p * rows_z + r] = found
        top[...] = jnp.maximum(
            top[...], jnp.maximum(found[:, :tokens], found[:, tokens:])
        )

    def kv_steps(t, carry):
        k_chain.step(t)
        v_chain.step(t)

        def way(d, carry):
            r = z + (1 - 2 * d) * (t - 1)
            fits = jnp.logical_and(r >= 0, r < rows_z)

            @pl.when(jnp.logical_and(fits, jnp.logical_or(t > 1, d == 0)))
            def _():
                score_unit(pair, r)

            return carry

        lax.fori_loop(0, 2, way, 0)
        return carry

    lax.fori_loop(1, rows_z + 1, kv_steps, 0)

    def from_sibling(r, carry):
        k_chain.copy(1 - pair, r, 2, sibling).wait_recv()
        score_unit(1 - pair, r)
        return carry

    lax.fori_loop(0, rows_z, from_sibling, 0)
    v_chain.sibling_recv()
    peak = jnp.max(top[...], axis=-1, keepdims=True)
    top[...] = jnp.broadcast_to(peak, top.shape)
    total[...] = jnp.zeros(total.shape, F32)
    mixed[...] = jnp.zeros(mixed.shape, F32)

    def mix_unit(u, carry):
        shift = top[...]
        left = jnp.exp(scores[u, :, 0:tokens] - shift)
        right = jnp.exp(scores[u, :, tokens : 2 * tokens] - shift)
        total[...] += left + right
        packed = values[u // rows_z, u % rows_z]
        stacked = jnp.concatenate([packed[:, :LAT], packed[:, LAT:]], axis=0)
        mixed[...] += jnp.dot(
            jnp.concatenate([left, right], axis=1).astype(BF16),
            stacked,
            preferred_element_type=F32,
        )
        return carry

    lax.fori_loop(0, 2 * rows_z, mix_unit, 0)
    attended = mixed[...] / jnp.sum(total[...], axis=-1, keepdims=True)
    share[...] = jnp.concatenate(
        [attended[: 2 * tokens], attended[2 * tokens :]], axis=1
    ).reshape(share.shape)

    for k in range(1, members):
        j, target = member(k)
        send(share.at[j], met.at[me], 6, target)
    met[me] = share[me]
    joined(met, 6, members - 1).wait_recv()
    halves[0] = jnp.sum(met[...], axis=0)
    send(halves.at[0], halves.at[1], 7, {"grp": (1 - z_hi) * 2 + core})
    joined(halves, 7, 1).wait_recv()
    shares = halves[0] + halves[1]
    taken_latent = latents[0, taken, :]
    taken_noisy = latents[1, taken, :]
    real = taken_noisy - level * (residual + shares[:, :LAT])
    fake_pred = taken_noisy - level * (residual + shares[:, LAT:])
    tiles[rank] = jnp.concatenate(
        [fake_pred - real, jnp.abs(taken_latent - real)], axis=1
    )
    for k in range(1, ranks):
        send(tiles.at[rank], tiles.at[rank], 8, fellow(k))
    joined(tiles, 8, ranks - 1).wait_recv()
    all_tiles = tiles[...]
    gap = jnp.sum(all_tiles, axis=0)
    gap = gap[0:8] + gap[8:16]
    lane = lax.broadcasted_iota(jnp.int32, gap.shape, 1)
    gap = jnp.where(lane >= LAT, gap, 0.0)
    diff = all_tiles.reshape(tokens, 128)[:, :LAT]

    grad_rows = grad_ref.shape[0]
    start, skip = group * grad_rows, 0
    if grad_rows % 128:
        skip = (group % 2) * LAT
        start = start - skip
    found = lax.dot_general(
        act_student[:, pl.ds(pl.multiple_of(start, 128), window.shape[0])],
        jnp.concatenate(three_parts(diff), axis=1),
        (((0,), (0,)), ((), ())),
        preferred_element_type=F32,
    )
    window[...] = found[:, :LAT] + found[:, LAT : 2 * LAT] + found[:, 2 * LAT :]
    quarter = grad_rows // 8
    for column in range(COLUMNS):
        low_rows = pl.multiple_of(skip + column * quarter, 8)
        high_rows = pl.multiple_of(skip + grad_rows // 2 + column * quarter, 8)
        y_out[column, 0:quarter, :] = jnp.concatenate(
            [window[pl.ds(low_rows, quarter), :], window[pl.ds(high_rows, quarter), :]],
            axis=1,
        )
        y_out[column, quarter : quarter + 8, :] = gap
    for k in range(1, COLUMNS):
        other, target = in_row(k)
        send(y_out.at[other], y_in.at[y], 9, target)
    y_in[y] = y_out[y]
    joined(y_in, 9, COLUMNS - 1).wait_recv()
    sums = jnp.sum(y_in[...], axis=0)
    owners = quarter // 8
    for r in range(rows_z):
        z_out[r, 0:8, :] = (
            sums[8 * r : 8 * r + 8] if r < owners else jnp.zeros((8, 128), F32)
        )
        z_out[r, 8:16, :] = sums[quarter:]
    for k in range(1, rows_z):
        other, target = in_column(k)
        send(z_out.at[other], z_in.at[z], 10, target)
    z_in[z] = z_out[z]
    joined(z_in, 10, rows_z - 1).wait_recv()
    sums = jnp.sum(z_in[...], axis=0)
    gap_total = jnp.sum(sums[8:16, :], keepdims=True)
    scale = 1.0 / (gap_total / (tokens * seqs * LAT) + 1e-05)
    token_scale = float(tokens * seqs) ** -0.5

    @pl.when(z < owners)
    def _():
        pieces[z] = (scale * token_scale) * sums[0:8, :]
        for k in range(1, rows_z):
            _, target = in_column(k)
            send(pieces.at[z], pieces.at[z], 11, target)
        if owners > 1:
            joined(pieces, 11, owners - 1).wait_recv()

    if owners < rows_z:

        @pl.when(z >= owners)
        def _():
            joined(pieces, 11, owners).wait_recv()

    columns[y] = pieces[...].reshape(quarter, 128)
    for k in range(1, COLUMNS):
        _, target = in_row(k)
        send(columns.at[y], columns.at[y], 12, target)
    diff_ref[...] = scale * diff
    joined(columns, 12, COLUMNS - 1).wait_recv()
    complete = columns[...].reshape(grad_rows // 2, 128)
    grad_ref[0 : grad_rows // 2, :] = complete[:, :LAT]
    grad_ref[grad_rows // 2 :, :] = complete[:, LAT:]

    copy_to(qk_staged, qk_staged, one_send.at[0], one_recv.at[0], here).wait_send()
    copy_to(vd_staged, vd_mail, one_send.at[1], one_recv.at[1], here).wait_send()
    joined(fold_column, 2, COLUMNS - 1).wait_send()
    joined(fold_rows, 3, rows_z - 1).wait_send()
    joined(fold_whole, 4, rows_z - 1).wait_send()
    joined(act, 5, 1).wait_send()
    joined(share, 6, members - 1).wait_send()
    joined(halves, 7, 1).wait_send()
    joined(tiles, 8, ranks - 1).wait_send()
    joined(y_out, 9, COLUMNS - 1).wait_send()
    joined(z_out, 10, rows_z - 1).wait_send()

    @pl.when(z < owners)
    def _():
        for _ in range(1, rows_z):
            joined(pieces, 11, 1).wait_send()

    joined(columns, 12, COLUMNS - 1).wait_send()
    qk.drain()
    dv.drain()
    k_chain.drain()
    v_chain.drain()


def local(
    student_hidden_states,
    student_norm_gain,
    student_output_head,
    noise,
    timestep,
    context,
    patch_embedding_input,
    attention_norm_gain,
    query_weight,
    key_weight,
    value_weight,
    adapter_down_weight,
    adapter_up_weight,
    output_weight,
    velocity_head_output,
):
    tokens, width = student_hidden_states.shape
    depth = query_weight.shape[0]
    seqs = lax.axis_size("seq")
    rows_z = seqs // COLUMNS
    groups = lax.axis_size("grp") * lax.axis_size("tp")
    ranks = 2 * lax.axis_size("tp")
    grad_rows = width // groups
    window = grad_rows + LAT if grad_rows % 128 else grad_rows
    quarter = grad_rows // 8
    vmem = pl.BlockSpec(memory_space=pltpu.VMEM)
    smem = pl.BlockSpec(memory_space=pltpu.SMEM)
    dma = pltpu.SemaphoreType.DMA
    chain = [dma((3 * rows_z,)), dma((2 * rows_z,))]
    return pl.pallas_call(
        functools.partial(kernel, rows_z),
        out_shape=(
            jax.ShapeDtypeStruct((tokens, LAT), F32),
            jax.ShapeDtypeStruct((grad_rows, LAT), F32),
        ),
        in_specs=[smem] + [vmem] * 14,
        out_specs=(vmem, vmem),
        scratch_shapes=[
            pltpu.VMEM((COLUMNS, rows_z, depth, 256), BF16),
            pltpu.VMEM((COLUMNS, rows_z, depth, 128), BF16),
            pltpu.VMEM((depth, 256), BF16),
            pltpu.VMEM((depth, 256), BF16),
            pltpu.VMEM((depth, 256), BF16),
            pltpu.VMEM((256 if depth % 128 else depth, 256), BF16),
            pltpu.VMEM((2, LAT, HEAD_WIDTH), F32),
            pltpu.VMEM((COLUMNS, LAT, HEAD_WIDTH), F32),
            pltpu.VMEM((rows_z, LAT // rows_z, HEAD_WIDTH), F32),
            pltpu.VMEM((rows_z, LAT // rows_z, HEAD_WIDTH), F32),
            pltpu.VMEM((rows_z, LAT // rows_z, HEAD_WIDTH), F32),
            pltpu.VMEM((tokens, width), BF16),
            pltpu.VMEM((tokens, width), F32),
            pltpu.VMEM((2, tokens, width), BF16),
            pltpu.VMEM((2, tokens, LAT), F32),
            pltpu.VMEM((2 * tokens, 256), F32),
            pltpu.VMEM((2 * tokens, 128), F32),
            pltpu.VMEM((2, rows_z, 2 * tokens, HEAD_WIDTH), BF16),
            pltpu.VMEM((2, rows_z, tokens, 128), BF16),
            pltpu.VMEM((2 * rows_z, 4 * tokens, 2 * tokens), F32),
            pltpu.VMEM((4 * tokens, tokens), F32),
            pltpu.VMEM((4 * tokens, tokens), F32),
            pltpu.VMEM((4 * tokens, LAT), F32),
            pltpu.VMEM((2 * ranks, 16, 128), F32),
            pltpu.VMEM((2 * ranks, 16, 128), F32),
            pltpu.VMEM((2, 16, 128), F32),
            pltpu.VMEM((ranks, 16, 128), F32),
            pltpu.VMEM((window, LAT), F32),
            pltpu.VMEM((COLUMNS, quarter + 8, 128), F32),
            pltpu.VMEM((COLUMNS, quarter + 8, 128), F32),
            pltpu.VMEM((rows_z, 16, 128), F32),
            pltpu.VMEM((rows_z, 16, 128), F32),
            pltpu.VMEM((quarter // 8, 8, 128), F32),
            pltpu.VMEM((COLUMNS, quarter, 128), F32),
        ]
        + chain * 4
        + [dma((13,)), dma((13,))],
        compiler_params=pltpu.CompilerParams(
            collective_id=0, has_side_effects=True, vmem_limit_bytes=52 * MIB
        ),
    )(
        timestep,
        student_hidden_states,
        student_norm_gain.reshape(1, width),
        student_output_head.T,
        noise.T,
        context,
        patch_embedding_input,
        attention_norm_gain.reshape(1, width),
        query_weight,
        key_weight,
        value_weight,
        adapter_down_weight.T,
        adapter_up_weight,
        output_weight.T,
        velocity_head_output.T,
    )


def solution(mesh):
    heads = P("seq", ("grp", "tp"))
    in_specs = (
        P("seq", None),
        P(),
        P(),
        P("seq", None),
        P(),
        P("seq", None),
        P(),
        P(),
        heads,
        heads,
        heads,
        P("seq", None),
        P(None, ("grp", "tp")),
        P(("grp", "tp"), "seq"),
        P(),
    )
    out_specs = (P("seq", None), P(("grp", "tp"), None))
    return jax.shard_map(local, mesh=mesh, in_specs=in_specs, out_specs=out_specs, check_vma=False)
```

time: 2180 us -> 154 us (0.07)
  waiting for transfers between devices: 1870 us -> 0 us
  blocking collectives: 238 us -> 0 us
  Pallas kernels: 0 us -> 140 us
  matrix products: 25.2 us -> 0 us
    all_gather x6 -> x0, waiting for transfers between devices: 1210 us -> none  [the longest x1 228 us: local(): lax.all_gather(value_weight, 'seq', axis=0, tiled=True)]
    psum x2 -> x0, waiting for transfers between devices: 659 us -> none  [the longest x1 399 us: local(): grad_total, gap_total = lax.psum((grad_part, gap_part), 'seq')]
    pallas_call x0 -> x1, Pallas kernels: none -> 140 us  [local(): pl.pallas_call(functools.partial(kernel, rows_z), out_shape=(jax.ShapeDty...]
    all_gather x1 -> x0, blocking collectives: 124 us -> none  [local(): lax.all_gather(adapter_down_weight, 'seq', axis=0, tiled=True)]
    psum x1 -> x0, blocking collectives: 113 us -> none  [local(): grad_total, gap_total = lax.psum((grad_part, gap_part), 'seq')]
    dot_general x12 -> x0, matrix products: 25.2 us -> none  [the longest x3 8 us: local(): jnp.dot(activation, block, preferred_element_type=jnp.float32)]
  transfers between devices with their start and end apart: 8 -> 0, of which waited for: 8 -> 0; matrix products, arithmetic and copies ran while one was open for 1% -> 0% of each run, Pallas kernels for 0% -> 0%
where the time goes in v2:
time: 154 us; the launch traced here: 153 us
  Pallas kernels  140 us (91%)
  local copies, waits for them, and re-layouts  10.9 us (7%)
    pallas_call x1, Pallas kernels, local(): pl.pallas_call(functools.partial(kernel, rows_z), out_shape=(jax.ShapeDty...  140 us
    unnamed x22, local copies, waits for them, and re-layouts  9.4 us

profile of v2, /device:TPU:24, one launch (start us, length us, event | category | flops | bytes accessed | tf_op | source)
XLA Modules:
  0.0 152.6 jit_solution(7456296556705042990)
XLA Ops:
  1.3 0.0 copy-start
  1.3 1.1 copy-done
  2.4 0.0 copy-start.1
  2.4 1.1 copy-done.1
  3.5 0.0 copy-start.2
  3.5 0.9 copy-done.2
  4.3 0.0 copy-start.3
  4.3 0.9 copy-done.3
  5.2 0.0 copy-start.4
  5.2 0.9 copy-done.4
  6.1 0.0 copy-start.5
  6.1 0.9 copy-done.5
  7.0 0.0 copy-start.6
  7.0 0.8 copy-done.6
  7.8 0.0 copy-start.7
  7.8 0.8 copy-done.7
  8.5 0.0 copy-start.8
  8.5 0.7 copy-done.8
  9.3 0.0 copy-start.9
  9.3 0.7 copy-done.9
  10.0 0.0 copy-start.10
  10.0 0.7 copy-done.10
  10.7 140.5 %shard_map.158 = (f32[128,64]{1,0:T(8,128)S(1)}, f32[320,64]{1,0:T(8,128)S(1)}) custom-call(s32[1]{0:T(128)S(6)} %copy.19.timestep_ref, bf16[128,5120]{1,0:T(8,128)(2,1)} %student_ref.1, f32[1,5120]{1,0:T(1,128)S(1)} %bitcast.10, bf16[64,5120]{1,0:T(8,128)(2,1)S(1)} %bitcast.7, bf16[64,128]{1,0:T(8,128)(2,1)S(1)} %bitcast.12, bf16[128,5120]{1,0:T(8,128)(2,1)} %context_ref.1, ...), custom_call_target="tpu_custom_call" | custom-call | tf_op jit(solution)/shard_map/pallas_call | solution.py:650
  151.2 0.7 copy.17
  151.9 0.8 copy.18
Async XLA Ops:
  1.3 1.1 copy-start
  2.4 1.1 copy-start.1
  3.5 0.9 copy-start.2
  4.3 0.9 copy-start.3
  5.2 0.9 copy-start.4
  6.1 0.9 copy-start.5
  7.0 0.8 copy-start.6
  7.8 0.8 copy-start.7
  8.5 0.7 copy-start.8
  9.3 0.7 copy-start.9
  10.0 0.7 copy-start.10

commit v3 on v2

--- a/solution.py
+++ b/solution.py
@@ -147,6 +147,22 @@
 def kernel(
     rows_z,
     timestep_ref,
+    student_hbm,
+    student_gain_hbm,
+    student_head_hbm,
+    noise_hbm,
+    context_hbm,
+    patch_hbm,
+    gain_hbm,
+    query_hbm,
+    key_hbm,
+    value_hbm,
+    down_hbm,
+    up_hbm,
+    output_hbm,
+    velocity_hbm,
+    diff_ref,
+    grad_ref,
     student_ref,
     student_gain_ref,
     student_head_ref,
@@ -154,20 +170,17 @@
     context_ref,
     patch_ref,
     gain_ref,
-    query_ref,
-    key_ref,
-    value_ref,
-    down_ref,
     up_ref,
     output_ref,
     velocity_ref,
-    diff_ref,
-    grad_ref,
-    qk_weights,
-    dv_weights,
-    qk_staged,
-    vd_staged,
-    vd_mail,
+    down_own,
+    down_mail,
+    value_own,
+    value_mail,
+    k_weights,
+    q_weights,
+    v_weights,
+    down_weights,
     placed,
     fold_out,
     fold_column,
@@ -178,8 +191,10 @@
     hidden,
     act,
     latents,
-    first,
-    second,
+    k_product,
+    q_product,
+    v_product,
+    low_product,
     keys,
     values,
     scores,
@@ -197,20 +212,27 @@
     z_in,
     pieces,
     columns,
-    qk_send,
-    qk_recv,
-    dv_send,
-    dv_recv,
-    k_send,
-    k_recv,
+    kw_send,
+    kw_recv,
+    qw_send,
+    qw_recv,
+    vw_send,
+    vw_recv,
+    dw_send,
+    dw_recv,
+    ka_send,
+    ka_recv,
+    kb_send,
+    kb_recv,
     v_send,
     v_recv,
     one_send,
     one_recv,
+    load_sem,
 ):
     seq, y, z, side, pair, partner, sibling = position(rows_z)
     tokens, width = student_ref.shape
-    depth = query_ref.shape[0]
+    depth = query_hbm.shape[0]
     tp_size = lax.axis_size("tp")
     tp = lax.axis_index("tp")
     grp = lax.axis_index("grp")
@@ -254,6 +276,32 @@
     def send(src, dst, sem, target):
         copy_to(src, dst, one_send.at[sem], one_recv.at[sem], target).start()
 
+    own_columns = pl.ds(pl.multiple_of(side * HEAD_WIDTH, HEAD_WIDTH), HEAD_WIDTH)
+    other_columns = pl.ds(pl.multiple_of((1 - side) * HEAD_WIDTH, HEAD_WIDTH), HEAD_WIDTH)
+    mine = 2 * pair + side
+    theirs = 2 * pair + 1 - side
+    sources = (
+        (output_hbm, output_ref),
+        (velocity_hbm, velocity_ref),
+        (student_hbm, student_ref),
+        (student_gain_hbm, student_gain_ref),
+        (key_hbm.at[:, own_columns], k_weights.at[mine, z]),
+        (query_hbm.at[:, own_columns], q_weights.at[mine, z]),
+        (student_head_hbm, student_head_ref),
+        (noise_hbm, noise_ref),
+        (patch_hbm, patch_ref),
+        (context_hbm, context_ref),
+        (gain_hbm, gain_ref),
+        (value_hbm.at[:, own_columns], value_own),
+        (down_hbm, down_own),
+        (up_hbm, up_ref),
+    )
+    loads = [
+        pltpu.make_async_copy(src, dst, load_sem.at[i]) for i, (src, dst) in enumerate(sources)
+    ]
+    for load in loads:
+        load.start()
+
     barrier = pltpu.get_barrier_semaphore()
 
     def greet(target):
@@ -270,6 +318,8 @@
             greet(member(k)[1])
     greet({"grp": (1 - z_hi) * 2 + core})
 
+    loads[0].wait()
+    loads[1].wait()
     wide = placed.shape[0]
     begin = seq * depth
     offset = begin % 128
@@ -283,25 +333,18 @@
     fold_out[0] = folded[:, :HEAD_WIDTH]
     fold_out[1] = folded[:, HEAD_WIDTH:]
     fold_column[y] = fold_out[side]
-    down = down_ref[...].astype(F32).T.astype(BF16)
-    own_columns = pl.ds(pl.multiple_of(side * HEAD_WIDTH, HEAD_WIDTH), HEAD_WIDTH)
-    other_columns = pl.ds(pl.multiple_of((1 - side) * HEAD_WIDTH, HEAD_WIDTH), HEAD_WIDTH)
-    mine = 2 * pair + side
-    theirs = 2 * pair + 1 - side
-    qk_weights[mine, z, :, 0:128] = query_ref[:, own_columns]
-    qk_weights[mine, z, :, 128:256] = key_ref[:, own_columns]
-    qk_staged[:, 0:128] = query_ref[:, other_columns]
-    qk_staged[:, 128:256] = key_ref[:, other_columns]
-    vd_staged[:, 0:128] = value_ref[:, other_columns]
-    vd_staged[:, 128:256] = jnp.concatenate([down, down], axis=1)
 
     pl.semaphore_wait(barrier, 1 + COLUMNS - 1 + rows_z - 1 + members - 2)
 
-    send(qk_staged, qk_weights.at[mine, z], 0, here)
-    send(vd_staged, vd_mail, 1, here)
+    send(key_hbm.at[:, other_columns], k_weights.at[mine, z], 0, here)
     for k in range(1, COLUMNS):
         other, target = in_row(k)
         send(fold_out.at[other // 2], fold_column.at[y], 2, target)
+    send(query_hbm.at[:, other_columns], q_weights.at[mine, z], 13, here)
+    send(value_hbm.at[:, other_columns], value_mail, 1, here)
+    send(down_hbm, down_mail, 14, here)
+    loads[2].wait()
+    loads[3].wait()
 
     chunk = 16
 
@@ -314,12 +357,19 @@
 
     lax.fori_loop(0, tokens // chunk, student_rows, 0)
 
-    copy_to(
-        qk_staged, qk_weights.at[theirs, z], one_send.at[0], one_recv.at[0], here
-    ).wait_recv()
-    qk = Chain(lambda p, r: qk_weights.at[pl.ds(2 * p, 2), r], qk_send, qk_recv, rows_z)
-    dv = Chain(lambda p, r: dv_weights.at[pl.ds(2 * p, 2), r], dv_send, dv_recv, rows_z)
-    qk.own()
+    def came(src, dst, sem):
+        copy_to(src, dst, one_send.at[sem], one_recv.at[sem], here).wait_recv()
+
+    def two_slots(ref):
+        return lambda p, r: ref.at[pl.ds(2 * p, 2), r]
+
+    kw = Chain(two_slots(k_weights), kw_send, kw_recv, rows_z)
+    qw = Chain(two_slots(q_weights), qw_send, qw_recv, rows_z)
+    vw = Chain(lambda p, r: v_weights.at[p, r], vw_send, vw_recv, rows_z)
+    dw = Chain(lambda p, r: down_weights.at[p, r], dw_send, dw_recv, rows_z)
+    loads[4].wait()
+    came(key_hbm.at[:, other_columns], k_weights.at[theirs, z], 0)
+    kw.own()
 
     joined(fold_column, 2, COLUMNS - 1).wait_recv()
     fold_rows[...] = jnp.sum(fold_column[...], axis=0).reshape(fold_rows.shape)
@@ -327,6 +377,11 @@
     for k in range(1, rows_z):
         other, target = in_column(k)
         send(fold_rows.at[other], fold_arrived.at[z], 3, target)
+    loads[5].wait()
+    came(query_hbm.at[:, other_columns], q_weights.at[theirs, z], 13)
+    qw.own()
+    loads[6].wait()
+    loads[7].wait()
 
     level = noise_level_of(timestep_ref)
     latent = lax.dot_general(
@@ -337,6 +392,8 @@
     )
     noise = noise_ref[...].astype(F32).T
     noisy = ((1.0 - level) * latent + level * noise).astype(BF16)
+    loads[8].wait()
+    loads[9].wait()
     slab = 512 if width % 512 == 0 else width
 
     def hidden_columns(i, carry):
@@ -348,12 +405,13 @@
 
     lax.fori_loop(0, width // slab, hidden_columns, 0)
 
+    kw.step(1)
     joined(fold_arrived, 3, rows_z - 1).wait_recv()
     fold_whole[z] = jnp.sum(fold_arrived[...], axis=0)
     for k in range(1, rows_z):
         other, target = in_column(k)
         send(fold_whole.at[z], fold_whole.at[z], 4, target)
-    qk.step(1)
+    loads[10].wait()
 
     def act_rows(i, carry):
         rows = pl.ds(pl.multiple_of(i * chunk, chunk), chunk)
@@ -363,25 +421,41 @@
         return carry
 
     lax.fori_loop(0, tokens // chunk, act_rows, 0)
-    send(act.at[side], act.at[side], 5, here)
+    half = tokens // 2
+    this_half = pl.ds(pl.multiple_of(core * half, half), half)
+    that_half = pl.ds(pl.multiple_of((1 - core) * half, half), half)
+    send(act.at[side, this_half], act.at[side, this_half], 5, here)
+    qw.step(1)
+    kw.step(2)
 
     joined(fold_whole, 4, rows_z - 1).wait_recv()
     whole = fold_whole[...].reshape(LAT, HEAD_WIDTH)
     high = whole.astype(BF16)
     rest = (whole - high.astype(F32)).astype(BF16)
     split = jnp.concatenate([high, rest], axis=0)
-    copy_to(vd_staged, vd_mail, one_send.at[1], one_recv.at[1], here).wait_recv()
-    for place, value, lower in (
-        (mine, value_ref[:, own_columns], down),
-        (theirs, vd_mail[:, 0:128], vd_mail[:, 128 : 128 + LAT]),
-    ):
+    loads[11].wait()
+    came(value_hbm.at[:, other_columns], value_mail, 1)
+
+    def fold_value(ref):
         moved = lax.dot_general(
-            value, split, (((1,), (1,)), ((), ())), preferred_element_type=F32
-        )
-        moved = (moved[:, :LAT] + moved[:, LAT:]).astype(BF16)
-        dv_weights[place, z] = jnp.concatenate([lower, moved], axis=1)
-    dv.own()
-    qk.step(2)
+            ref[...], split, (((1,), (1,)), ((), ())), preferred_element_type=F32
+        )
+        return moved[:, :LAT] + moved[:, LAT:]
+
+    def in_order(own, other):
+        lower = jnp.where(side == 0, own, other)
+        upper = jnp.where(side == 0, other, own)
+        return jnp.concatenate([lower, upper], axis=1).astype(BF16)
+
+    v_weights[pair, z] = in_order(fold_value(value_own), fold_value(value_mail))
+    vw.own()
+    loads[12].wait()
+    came(down_hbm, down_mail, 14)
+    down_weights[pair, z] = in_order(
+        down_own[...].astype(F32).T, down_mail[...].astype(F32).T
+    )
+    dw.own()
+    qw.step(2)
 
     taken = pl.ds(pl.multiple_of(rank * 16, 16), 16)
     latents[0] = latent
@@ -392,45 +466,60 @@
     )
     residual = residual[0:16] + residual[16:32] + residual[32:48]
 
-    def both_steps(t, carry):
-        dv.step(t)
-        qk.step(t + 2)
+    def weight_steps(t, carry):
+        kw.step(t + 2)
+        vw.step(t)
+        qw.step(t + 2)
+        dw.step(t)
         return carry
 
-    lax.fori_loop(1, rows_z, both_steps, 0)
-    copy_to(
-        act.at[1 - side], act.at[1 - side], one_send.at[5], one_recv.at[5], here
-    ).wait_recv()
-
-    def project(place, column, fresh):
+    middle = min(4, rows_z)
+    lax.fori_loop(1, middle, weight_steps, 0)
+    came(act.at[1 - side, this_half], act.at[1 - side, this_half], 5)
+    core_mate = {"grp": grp + 1 - 2 * core}
+    send(act.at[1 - side, this_half], act.at[1 - side, this_half], 15, core_mate)
+    lax.fori_loop(middle, rows_z, weight_steps, 0)
+    came(act.at[1 - side, that_half], act.at[1 - side, that_half], 15)
+
+    def rows_at(column):
         part = pl.ds(pl.multiple_of(column * span, span), span)
-        rows = act[:, :, part].reshape(2 * tokens, span)
-        one = jnp.dot(
-            rows, qk_weights[place].reshape(span, 256), preferred_element_type=F32
-        )
-        two = jnp.dot(
-            rows, dv_weights[place].reshape(span, 128), preferred_element_type=F32
-        )
-        first[...] = one if fresh else first[...] + one
-        second[...] = two if fresh else second[...] + two
-
-    project(2 * pair, pair, True)
-    project(2 * pair + 1, 3 - pair, False)
-    qk.sibling_recv()
-    dv.sibling_recv()
-    project(2 - 2 * pair, 1 - pair, False)
-    project(3 - 2 * pair, 2 + pair, False)
-
-    keys[pair, z] = first[:, 128:256].astype(BF16)
-    k_chain = Chain(lambda p, r: keys.at[p, r], k_send, k_recv, rows_z)
-    v_chain = Chain(lambda p, r: values.at[p, r], v_send, v_recv, rows_z)
-    k_chain.own()
-    moved = second[:, LAT:].astype(BF16)
+        return act[:, :, part].reshape(2 * tokens, span)
+
+    def project(weights, p):
+        lower = jnp.dot(
+            rows_at(p), weights[2 * p].reshape(span, 128), preferred_element_type=F32
+        )
+        upper = jnp.dot(
+            rows_at(3 - p), weights[2 * p + 1].reshape(span, 128), preferred_element_type=F32
+        )
+        return lower + upper
+
+    def project_packed(weights, p):
+        packed = weights[p].reshape(span, 128)
+        lower = jnp.dot(rows_at(p), packed, preferred_element_type=F32)
+        upper = jnp.dot(rows_at(3 - p), packed, preferred_element_type=F32)
+        return lower[:, :LAT] + upper[:, LAT:]
+
+    k_product[...] = project(k_weights, pair)
+    kw.sibling_recv()
+    keys[pair, z] = (k_product[...] + project(k_weights, 1 - pair)).astype(BF16)
+    ka = Chain(lambda p, r: keys.at[p, r, pl.ds(0, tokens)], ka_send, ka_recv, rows_z)
+    kb = Chain(lambda p, r: keys.at[p, r, pl.ds(tokens, tokens)], kb_send, kb_recv, rows_z)
+    vs = Chain(lambda p, r: values.at[p, r], v_send, v_recv, rows_z)
+    ka.own()
+    kb.own()
+    v_product[...] = project_packed(v_weights, pair)
+    vw.sibling_recv()
+    moved = (v_product[...] + project_packed(v_weights, 1 - pair)).astype(BF16)
     values[pair, z] = jnp.concatenate([moved[:tokens], moved[tokens:]], axis=1)
-    v_chain.own()
-
-    low = second[:, :LAT].astype(BF16)
-    plain = first[:, 0:128]
+    vs.own()
+    q_product[...] = project(q_weights, pair)
+    low_product[...] = project_packed(down_weights, pair)
+    qw.sibling_recv()
+    plain = q_product[...] + project(q_weights, 1 - pair)
+    dw.sibling_recv()
+    low = (low_product[...] + project_packed(down_weights, 1 - pair)).astype(BF16)
+    loads[13].wait()
     fake = plain + jnp.dot(low, up_ref[:, own_columns], preferred_element_type=F32)
     asked = jnp.concatenate([plain, fake], axis=0).astype(BF16)
     top[...] = jnp.full(top.shape, -1e30, F32)
@@ -449,8 +538,9 @@
         )
 
     def kv_steps(t, carry):
-        k_chain.step(t)
-        v_chain.step(t)
+        ka.step(t)
+        kb.step(t)
+        vs.step(t)
 
         def way(d, carry):
             r = z + (1 - 2 * d) * (t - 1)
@@ -468,12 +558,13 @@
     lax.fori_loop(1, rows_z + 1, kv_steps, 0)
 
     def from_sibling(r, carry):
-        k_chain.copy(1 - pair, r, 2, sibling).wait_recv()
+        ka.copy(1 - pair, r, 2, sibling).wait_recv()
+        kb.copy(1 - pair, r, 2, sibling).wait_recv()
         score_unit(1 - pair, r)
         return carry
 
     lax.fori_loop(0, rows_z, from_sibling, 0)
-    v_chain.sibling_recv()
+    vs.sibling_recv()
     peak = jnp.max(top[...], axis=-1, keepdims=True)
     top[...] = jnp.broadcast_to(peak, top.shape)
     total[...] = jnp.zeros(total.shape, F32)
@@ -593,12 +684,18 @@
     grad_ref[0 : grad_rows // 2, :] = complete[:, :LAT]
     grad_ref[grad_rows // 2 :, :] = complete[:, LAT:]
 
-    copy_to(qk_staged, qk_staged, one_send.at[0], one_recv.at[0], here).wait_send()
-    copy_to(vd_staged, vd_mail, one_send.at[1], one_recv.at[1], here).wait_send()
+    def left(src, dst, sem):
+        copy_to(src, dst, one_send.at[sem], one_recv.at[sem], here).wait_send()
+
+    left(key_hbm.at[:, other_columns], k_weights.at[mine, z], 0)
+    left(query_hbm.at[:, other_columns], q_weights.at[mine, z], 13)
+    left(value_hbm.at[:, other_columns], value_mail, 1)
+    left(down_hbm, down_mail, 14)
+    left(act.at[side, this_half], act.at[side, this_half], 5)
+    left(act.at[1 - side, this_half], act.at[1 - side, this_half], 15)
     joined(fold_column, 2, COLUMNS - 1).wait_send()
     joined(fold_rows, 3, rows_z - 1).wait_send()
     joined(fold_whole, 4, rows_z - 1).wait_send()
-    joined(act, 5, 1).wait_send()
     joined(share, 6, members - 1).wait_send()
     joined(halves, 7, 1).wait_send()
     joined(tiles, 8, ranks - 1).wait_send()
@@ -611,10 +708,8 @@
             joined(pieces, 11, 1).wait_send()
 
     joined(columns, 12, COLUMNS - 1).wait_send()
-    qk.drain()
-    dv.drain()
-    k_chain.drain()
-    v_chain.drain()
+    for chain in (kw, qw, vw, dw, ka, kb, vs):
+        chain.drain()
 
 
 def local(
@@ -653,14 +748,27 @@
             jax.ShapeDtypeStruct((tokens, LAT), F32),
             jax.ShapeDtypeStruct((grad_rows, LAT), F32),
         ),
-        in_specs=[smem] + [vmem] * 14,
+        in_specs=[smem] + [pl.BlockSpec(memory_space=pl.ANY)] * 14,
         out_specs=(vmem, vmem),
         scratch_shapes=[
-            pltpu.VMEM((COLUMNS, rows_z, depth, 256), BF16),
-            pltpu.VMEM((COLUMNS, rows_z, depth, 128), BF16),
-            pltpu.VMEM((depth, 256), BF16),
-            pltpu.VMEM((depth, 256), BF16),
-            pltpu.VMEM((depth, 256), BF16),
+            pltpu.VMEM((tokens, width), BF16),
+            pltpu.VMEM((1, width), F32),
+            pltpu.VMEM((LAT, width), BF16),
+            pltpu.VMEM((LAT, tokens), BF16),
+            pltpu.VMEM((tokens, width), BF16),
+            pltpu.VMEM((LAT, width), BF16),
+            pltpu.VMEM((1, width), F32),
+            pltpu.VMEM(adapter_up_weight.shape, BF16),
+            pltpu.VMEM((depth, 2 * HEAD_WIDTH), BF16),
+            pltpu.VMEM((LAT, width), BF16),
+            pltpu.VMEM((LAT, depth), BF16),
+            pltpu.VMEM((LAT, depth), BF16),
+            pltpu.VMEM((depth, HEAD_WIDTH), BF16),
+            pltpu.VMEM((depth, HEAD_WIDTH), BF16),
+            pltpu.VMEM((COLUMNS, rows_z, depth, HEAD_WIDTH), BF16),
+            pltpu.VMEM((COLUMNS, rows_z, depth, HEAD_WIDTH), BF16),
+            pltpu.VMEM((2, rows_z, depth, 2 * LAT), BF16),
+            pltpu.VMEM((2, rows_z, depth, 2 * LAT), BF16),
             pltpu.VMEM((256 if depth % 128 else depth, 256), BF16),
             pltpu.VMEM((2, LAT, HEAD_WIDTH), F32),
             pltpu.VMEM((COLUMNS, LAT, HEAD_WIDTH), F32),
@@ -671,8 +779,10 @@
             pltpu.VMEM((tokens, width), F32),
             pltpu.VMEM((2, tokens, width), BF16),
             pltpu.VMEM((2, tokens, LAT), F32),
-            pltpu.VMEM((2 * tokens, 256), F32),
-            pltpu.VMEM((2 * tokens, 128), F32),
+            pltpu.VMEM((2 * tokens, HEAD_WIDTH), F32),
+            pltpu.VMEM((2 * tokens, HEAD_WIDTH), F32),
+            pltpu.VMEM((2 * tokens, LAT), F32),
+            pltpu.VMEM((2 * tokens, LAT), F32),
             pltpu.VMEM((2, rows_z, 2 * tokens, HEAD_WIDTH), BF16),
             pltpu.VMEM((2, rows_z, tokens, 128), BF16),
             pltpu.VMEM((2 * rows_z, 4 * tokens, 2 * tokens), F32),
@@ -691,10 +801,10 @@
             pltpu.VMEM((quarter // 8, 8, 128), F32),
             pltpu.VMEM((COLUMNS, quarter, 128), F32),
         ]
-        + chain * 4
-        + [dma((13,)), dma((13,))],
+        + chain * 7
+        + [dma((16,)), dma((16,)), dma((14,))],
         compiler_params=pltpu.CompilerParams(
-            collective_id=0, has_side_effects=True, vmem_limit_bytes=52 * MIB
+            collective_id=0, has_side_effects=True, vmem_limit_bytes=60 * MIB
         ),
     )(
         timestep,

time: 154 us -> 139 us (0.903)
  local copies, waits for them, and re-layouts: 10.9 us -> 3.21 us
  Pallas kernels: 140 us -> 134 us
    unnamed x22 -> x0, local copies, waits for them, and re-layouts: 9.4 us -> none
    pallas_call x1, Pallas kernels: 140 us -> 134 us  [local(): pl.pallas_call(functools.partial(kernel, rows_z), out_shape=(jax.ShapeDty...]
    pallas_call x2, local copies, waits for them, and re-layouts: 1.45 us -> 3.21 us  [local(): pl.pallas_call(functools.partial(kernel, rows_z), out_shape=(jax.ShapeDty...]
where the time goes in v3:
time: 139 us; the launch traced here: 138 us
  Pallas kernels  134 us (96%)
  local copies, waits for them, and re-layouts  3.21 us (2%)
    pallas_call x1, Pallas kernels, local(): pl.pallas_call(functools.partial(kernel, rows_z), out_shape=(jax.ShapeDty...  134 us
    pallas_call x2, local copies, waits for them, and re-layouts, local(): pl.pallas_call(functools.partial(kernel, rows_z), out_shape=(jax.ShapeDty...  3.21 us

profile of v3, /device:TPU:24, one launch (start us, length us, event | category | flops | bytes accessed | tf_op | source)
XLA Modules:
  0.0 138.1 jit_solution(7633955750138579481)
XLA Ops:
  1.3 133.6 %shard_map.158 = (f32[128,64]{1,0:T(8,128)}, f32[320,64]{1,0:T(8,128)}) custom-call(s32[1]{0:T(128)S(6)} %copy.19.timestep_ref, bf16[128,5120]{1,0:T(8,128)(2,1)} %student_hbm.1, f32[1,5120]{1,0:T(1,128)} %bitcast.11, bf16[64,5120]{1,0:T(8,128)(2,1)} %bitcast.7, bf16[64,128]{1,0:T(8,128)(2,1)} %bitcast.13, bf16[128,5120]{1,0:T(8,128)(2,1)} %context_hbm.1, ...), custom_call_target="tpu_custom_call" | custom-call | tf_op jit(solution)/shard_map/pallas_call | solution.py:745
  134.9 1.5 %copy.17 = f32[128,64]{0,1:T(8,128)} copy(f32[128,64]{1,0:T(8,128)} %get-tuple-element.2) | data formatting | bytes 65536 | tf_op jit(solution)/shard_map/pallas_call | solution.py:745
  136.4 1.7 %copy.18 = f32[320,64]{0,1:T(8,128)} copy(f32[320,64]{1,0:T(8,128)} %get-tuple-element.3) | data formatting | bytes 163840 | tf_op jit(solution)/shard_map/pallas_call | solution.py:745

commit v4 on v3

--- a/solution.py
+++ b/solution.py
@@ -38,9 +38,13 @@
 
 
 class Chain:
-    def __init__(self, unit, send_sem, recv_sem, rows_z):
+    def __init__(self, unit, send_sem, recv_sem, rows_z, only=None):
         self.unit, self.send_sem, self.recv_sem, self.rows_z = unit, send_sem, recv_sem, rows_z
+        self.only = only
         (self.seq, _, self.z, _, self.pair, _, self.sibling) = position(rows_z)
+
+    def moves(self, row, condition):
+        return condition if self.only is None else jnp.logical_and(condition, row == self.only)
 
     def copy(self, pair, row, way, target):
         ref = self.unit(pair, row)
@@ -64,20 +68,26 @@
     def own(self):
         z = self.z
 
-        @pl.when(z < self.rows_z - 1)
+        @pl.when(self.moves(z, z < self.rows_z - 1))
         def _():
             self.up(z).start()
 
-        @pl.when(z > 0)
+        @pl.when(self.moves(z, z > 0))
         def _():
             self.down(z).start()
 
-        self.across(z).start()
+        if self.only is None:
+            self.across(z).start()
+        else:
+
+            @pl.when(z == self.only)
+            def _():
+                self.across(z).start()
 
     def step(self, t):
         z, last = self.z, self.rows_z - 1
 
-        @pl.when(z - t >= 0)
+        @pl.when(self.moves(z - t, z - t >= 0))
         def _():
             row = z - t
             self.up(row).wait_recv()
@@ -88,7 +98,7 @@
 
             self.across(row).start()
 
-        @pl.when(z + t <= last)
+        @pl.when(self.moves(z + t, z + t <= last))
         def _():
             row = z + t
             self.down(row).wait_recv()
@@ -99,16 +109,12 @@
 
             self.across(row).start()
 
-    def forward(self):
-        def body(t, carry):
-            self.step(t)
-            return carry
-
-        lax.fori_loop(1, self.rows_z, body, 0)
-
     def sibling_recv(self):
         def body(row, carry):
-            self.copy(1 - self.pair, row, 2, self.sibling).wait_recv()
+            @pl.when(self.moves(row, row >= 0))
+            def _():
+                self.copy(1 - self.pair, row, 2, self.sibling).wait_recv()
+
             return carry
 
         lax.fori_loop(0, self.rows_z, body, 0)
@@ -117,15 +123,18 @@
         z, last = self.z, self.rows_z - 1
 
         def body(row, carry):
-            @pl.when(jnp.logical_and(z < last, row <= z))
+            @pl.when(self.moves(row, jnp.logical_and(z < last, row <= z)))
             def _():
                 self.up(row).wait_send()
 
-            @pl.when(jnp.logical_and(z > 0, row >= z))
+            @pl.when(self.moves(row, jnp.logical_and(z > 0, row >= z)))
             def _():
                 self.down(row).wait_send()
 
-            self.across(row).wait_send()
+            @pl.when(self.moves(row, row >= 0))
+            def _():
+                self.across(row).wait_send()
+
             return carry
 
         lax.fori_loop(0, self.rows_z, body, 0)
@@ -181,6 +190,7 @@
     q_weights,
     v_weights,
     down_weights,
+    down_placed,
     placed,
     fold_out,
     fold_column,
@@ -194,7 +204,9 @@
     k_product,
     q_product,
     v_product,
-    low_product,
+    low_out,
+    low_in,
+    low_tiles,
     keys,
     values,
     scores,
@@ -302,6 +314,46 @@
     for load in loads:
         load.start()
 
+    centre = rows_z // 2 - 1
+    own_part = jnp.clip(z - centre, 0, 1)
+    is_owner = jnp.logical_and(z >= centre, z <= centre + 1)
+
+    def to_owners(parts, arrived, sem):
+        for o in range(2):
+
+            @pl.when(z != centre + o)
+            def _():
+                send(parts.at[o], arrived.at[z], sem, {"seq": y * rows_z + centre + o})
+
+    def own_sum(parts, arrived, sem):
+        arrived[z] = parts[own_part]
+        joined(arrived, sem, rows_z - 1).wait_recv()
+        return jnp.sum(arrived[...], axis=0)
+
+    def from_owner(whole, sem):
+        for k in range(1, rows_z):
+            _, target = in_column(k)
+            send(whole.at[own_part], whole.at[own_part], sem, target)
+
+    def owners_done(whole, sem):
+        @pl.when(is_owner)
+        def _():
+            joined(whole, sem, 1).wait_recv()
+
+        @pl.when(jnp.logical_not(is_owner))
+        def _():
+            joined(whole, sem, 2).wait_recv()
+
+    def owners_left(parts, arrived, whole, first_sem, second_sem):
+        @pl.when(is_owner)
+        def _():
+            joined(parts, first_sem, 1).wait_send()
+            joined(arrived, second_sem, rows_z - 1).wait_send()
+
+        @pl.when(jnp.logical_not(is_owner))
+        def _():
+            joined(parts, first_sem, 2).wait_send()
+
     barrier = pltpu.get_barrier_semaphore()
 
     def greet(target):
@@ -366,20 +418,33 @@
     kw = Chain(two_slots(k_weights), kw_send, kw_recv, rows_z)
     qw = Chain(two_slots(q_weights), qw_send, qw_recv, rows_z)
     vw = Chain(lambda p, r: v_weights.at[p, r], vw_send, vw_recv, rows_z)
-    dw = Chain(lambda p, r: down_weights.at[p, r], dw_send, dw_recv, rows_z)
+    dw = Chain(lambda p, r: down_weights.at[p], dw_send, dw_recv, rows_z, rank)
     loads[4].wait()
     came(key_hbm.at[:, other_columns], k_weights.at[theirs, z], 0)
     kw.own()
 
     joined(fold_column, 2, COLUMNS - 1).wait_recv()
     fold_rows[...] = jnp.sum(fold_column[...], axis=0).reshape(fold_rows.shape)
-    fold_arrived[z] = fold_rows[z]
-    for k in range(1, rows_z):
-        other, target = in_column(k)
-        send(fold_rows.at[other], fold_arrived.at[z], 3, target)
+    to_owners(fold_rows, fold_arrived, 3)
     loads[5].wait()
     came(query_hbm.at[:, other_columns], q_weights.at[theirs, z], 13)
     qw.own()
+
+    def in_order(own, other):
+        lower = jnp.where(side == 0, own, other)
+        upper = jnp.where(side == 0, other, own)
+        return jnp.concatenate([lower, upper], axis=1).astype(BF16)
+
+    loads[12].wait()
+    came(down_hbm, down_mail, 14)
+
+    @pl.when(z == rank)
+    def _():
+        down_weights[pair] = in_order(
+            down_own[...].astype(F32).T, down_mail[...].astype(F32).T
+        )
+
+    dw.own()
     loads[6].wait()
     loads[7].wait()
 
@@ -406,11 +471,11 @@
     lax.fori_loop(0, width // slab, hidden_columns, 0)
 
     kw.step(1)
-    joined(fold_arrived, 3, rows_z - 1).wait_recv()
-    fold_whole[z] = jnp.sum(fold_arrived[...], axis=0)
-    for k in range(1, rows_z):
-        other, target = in_column(k)
-        send(fold_whole.at[z], fold_whole.at[z], 4, target)
+    @pl.when(is_owner)
+    def _():
+        fold_whole[own_part] = own_sum(fold_rows, fold_arrived, 3)
+        from_owner(fold_whole, 4)
+
     loads[10].wait()
 
     def act_rows(i, carry):
@@ -428,7 +493,7 @@
     qw.step(1)
     kw.step(2)
 
-    joined(fold_whole, 4, rows_z - 1).wait_recv()
+    owners_done(fold_whole, 4)
     whole = fold_whole[...].reshape(LAT, HEAD_WIDTH)
     high = whole.astype(BF16)
     rest = (whole - high.astype(F32)).astype(BF16)
@@ -442,19 +507,8 @@
         )
         return moved[:, :LAT] + moved[:, LAT:]
 
-    def in_order(own, other):
-        lower = jnp.where(side == 0, own, other)
-        upper = jnp.where(side == 0, other, own)
-        return jnp.concatenate([lower, upper], axis=1).astype(BF16)
-
     v_weights[pair, z] = in_order(fold_value(value_own), fold_value(value_mail))
     vw.own()
-    loads[12].wait()
-    came(down_hbm, down_mail, 14)
-    down_weights[pair, z] = in_order(
-        down_own[...].astype(F32).T, down_mail[...].astype(F32).T
-    )
-    dw.own()
     qw.step(2)
 
     taken = pl.ds(pl.multiple_of(rank * 16, 16), 16)
@@ -500,6 +554,31 @@
         upper = jnp.dot(rows_at(3 - p), packed, preferred_element_type=F32)
         return lower[:, :LAT] + upper[:, LAT:]
 
+    dw.sibling_recv()
+    row = jnp.minimum(rank, rows_z - 1)
+    shift = (row * depth) % 128
+    down_placed[...] = jnp.zeros(down_placed.shape, BF16)
+    for p in range(2):
+        down_placed[p, pl.ds(pl.multiple_of(shift, 32), depth), :] = down_weights[p]
+
+    def low_term(column, p):
+        part = pl.ds(pl.multiple_of(column * span + row * depth - shift, 128), wide)
+        rows = act[:, :, part].reshape(2 * tokens, wide)
+        return jnp.dot(rows, down_placed[p], preferred_element_type=F32)
+
+    low_sum = (
+        low_term(0, 0)[:, :LAT]
+        + low_term(3, 0)[:, LAT:]
+        + low_term(1, 1)[:, :LAT]
+        + low_term(2, 1)[:, LAT:]
+    )
+    low_sum = jnp.where(rank < rows_z, low_sum, 0.0)
+    low_out[...] = jnp.concatenate([low_sum[:tokens], low_sum[tokens:]], axis=1).reshape(
+        low_out.shape
+    )
+    for k in range(1, ranks):
+        send(low_out.at[(rank + k) % ranks], low_in.at[rank], 16, fellow(k))
+    low_in[rank] = low_out[rank]
     k_product[...] = project(k_weights, pair)
     kw.sibling_recv()
     keys[pair, z] = (k_product[...] + project(k_weights, 1 - pair)).astype(BF16)
@@ -508,17 +587,21 @@
     vs = Chain(lambda p, r: values.at[p, r], v_send, v_recv, rows_z)
     ka.own()
     kb.own()
+    joined(low_in, 16, ranks - 1).wait_recv()
+    low_tiles[rank] = jnp.sum(low_in[...], axis=0).astype(BF16)
+    for k in range(1, ranks):
+        send(low_tiles.at[rank], low_tiles.at[rank], 17, fellow(k))
     v_product[...] = project_packed(v_weights, pair)
     vw.sibling_recv()
     moved = (v_product[...] + project_packed(v_weights, 1 - pair)).astype(BF16)
     values[pair, z] = jnp.concatenate([moved[:tokens], moved[tokens:]], axis=1)
     vs.own()
     q_product[...] = project(q_weights, pair)
-    low_product[...] = project_packed(down_weights, pair)
     qw.sibling_recv()
     plain = q_product[...] + project(q_weights, 1 - pair)
-    dw.sibling_recv()
-    low = (low_product[...] + project_packed(down_weights, 1 - pair)).astype(BF16)
+    joined(low_tiles, 17, ranks - 1).wait_recv()
+    low = low_tiles[...].reshape(tokens, 2 * LAT)
+    low = jnp.concatenate([low[:, :LAT], low[:, LAT:]], axis=0)
     loads[13].wait()
     fake = plain + jnp.dot(low, up_ref[:, own_columns], preferred_element_type=F32)
     asked = jnp.concatenate([plain, fake], axis=0).astype(BF16)
@@ -643,38 +726,31 @@
     y_in[y] = y_out[y]
     joined(y_in, 9, COLUMNS - 1).wait_recv()
     sums = jnp.sum(y_in[...], axis=0)
-    owners = quarter // 8
-    for r in range(rows_z):
-        z_out[r, 0:8, :] = (
-            sums[8 * r : 8 * r + 8] if r < owners else jnp.zeros((8, 128), F32)
-        )
-        z_out[r, 8:16, :] = sums[quarter:]
-    for k in range(1, rows_z):
-        other, target = in_column(k)
-        send(z_out.at[other], z_in.at[z], 10, target)
-    z_in[z] = z_out[z]
-    joined(z_in, 10, rows_z - 1).wait_recv()
-    sums = jnp.sum(z_in[...], axis=0)
-    gap_total = jnp.sum(sums[8:16, :], keepdims=True)
-    scale = 1.0 / (gap_total / (tokens * seqs * LAT) + 1e-05)
+    share_rows = z_out.shape[1] - 8
+    z_out[0, 0:share_rows, :] = sums[0:share_rows]
+    z_out[1, 0 : quarter - share_rows, :] = sums[share_rows:quarter]
+    if quarter < 2 * share_rows:
+        z_out[1, quarter - share_rows : share_rows, :] = jnp.zeros(
+            (2 * share_rows - quarter, 128), F32
+        )
+    for o in range(2):
+        z_out[o, share_rows : share_rows + 8, :] = sums[quarter:]
+    to_owners(z_out, z_in, 10)
     token_scale = float(tokens * seqs) ** -0.5
 
-    @pl.when(z < owners)
+    @pl.when(is_owner)
     def _():
-        pieces[z] = (scale * token_scale) * sums[0:8, :]
-        for k in range(1, rows_z):
-            _, target = in_column(k)
-            send(pieces.at[z], pieces.at[z], 11, target)
-        if owners > 1:
-            joined(pieces, 11, owners - 1).wait_recv()
-
-    if owners < rows_z:
-
-        @pl.when(z >= owners)
-        def _():
-            joined(pieces, 11, owners).wait_recv()
-
-    columns[y] = pieces[...].reshape(quarter, 128)
+        summed = own_sum(z_out, z_in, 10)
+        gap_total = jnp.sum(summed[share_rows:], keepdims=True)
+        factor = 1.0 / (gap_total / (tokens * seqs * LAT) + 1e-05)
+        pieces[own_part, 0:share_rows, :] = (factor * token_scale) * summed[0:share_rows]
+        pieces[own_part, share_rows : share_rows + 8, :] = jnp.broadcast_to(factor, (8, 128))
+        from_owner(pieces, 11)
+
+    owners_done(pieces, 11)
+    scale = pieces[0, share_rows : share_rows + 1, 0:1]
+    columns[y, 0:share_rows, :] = pieces[0, 0:share_rows, :]
+    columns[y, share_rows:quarter, :] = pieces[1, 0 : quarter - share_rows, :]
     for k in range(1, COLUMNS):
         _, target = in_row(k)
         send(columns.at[y], columns.at[y], 12, target)
@@ -691,22 +767,17 @@
     left(query_hbm.at[:, other_columns], q_weights.at[mine, z], 13)
     left(value_hbm.at[:, other_columns], value_mail, 1)
     left(down_hbm, down_mail, 14)
+    joined(low_out, 16, ranks - 1).wait_send()
+    joined(low_tiles, 17, ranks - 1).wait_send()
     left(act.at[side, this_half], act.at[side, this_half], 5)
     left(act.at[1 - side, this_half], act.at[1 - side, this_half], 15)
     joined(fold_column, 2, COLUMNS - 1).wait_send()
-    joined(fold_rows, 3, rows_z - 1).wait_send()
-    joined(fold_whole, 4, rows_z - 1).wait_send()
+    owners_left(fold_rows, fold_arrived, fold_whole, 3, 4)
     joined(share, 6, members - 1).wait_send()
     joined(halves, 7, 1).wait_send()
     joined(tiles, 8, ranks - 1).wait_send()
     joined(y_out, 9, COLUMNS - 1).wait_send()
-    joined(z_out, 10, rows_z - 1).wait_send()
-
-    @pl.when(z < owners)
-    def _():
-        for _ in range(1, rows_z):
-            joined(pieces, 11, 1).wait_send()
-
+    owners_left(z_out, z_in, pieces, 10, 11)
     joined(columns, 12, COLUMNS - 1).wait_send()
     for chain in (kw, qw, vw, dw, ka, kb, vs):
         chain.drain()
@@ -738,6 +809,8 @@
     grad_rows = width // groups
     window = grad_rows + LAT if grad_rows % 128 else grad_rows
     quarter = grad_rows // 8
+    share_rows = (quarter // 8 + 1) // 2 * 8
+    wide = 256 if depth % 128 else depth
     vmem = pl.BlockSpec(memory_space=pltpu.VMEM)
     smem = pl.BlockSpec(memory_space=pltpu.SMEM)
     dma = pltpu.SemaphoreType.DMA
@@ -768,13 +841,14 @@
             pltpu.VMEM((COLUMNS, rows_z, depth, HEAD_WIDTH), BF16),
             pltpu.VMEM((COLUMNS, rows_z, depth, HEAD_WIDTH), BF16),
             pltpu.VMEM((2, rows_z, depth, 2 * LAT), BF16),
-            pltpu.VMEM((2, rows_z, depth, 2 * LAT), BF16),
-            pltpu.VMEM((256 if depth % 128 else depth, 256), BF16),
+            pltpu.VMEM((2, depth, 2 * LAT), BF16),
+            pltpu.VMEM((2, wide, 2 * LAT), BF16),
+            pltpu.VMEM((wide, 256), BF16),
             pltpu.VMEM((2, LAT, HEAD_WIDTH), F32),
             pltpu.VMEM((COLUMNS, LAT, HEAD_WIDTH), F32),
-            pltpu.VMEM((rows_z, LAT // rows_z, HEAD_WIDTH), F32),
-            pltpu.VMEM((rows_z, LAT // rows_z, HEAD_WIDTH), F32),
-            pltpu.VMEM((rows_z, LAT // rows_z, HEAD_WIDTH), F32),
+            pltpu.VMEM((2, LAT // 2, HEAD_WIDTH), F32),
+            pltpu.VMEM((rows_z, LAT // 2, HEAD_WIDTH), F32),
+            pltpu.VMEM((2, LAT // 2, HEAD_WIDTH), F32),
             pltpu.VMEM((tokens, width), BF16),
             pltpu.VMEM((tokens, width), F32),
             pltpu.VMEM((2, tokens, width), BF16),
@@ -782,7 +856,9 @@
             pltpu.VMEM((2 * tokens, HEAD_WIDTH), F32),
             pltpu.VMEM((2 * tokens, HEAD_WIDTH), F32),
             pltpu.VMEM((2 * tokens, LAT), F32),
-            pltpu.VMEM((2 * tokens, LAT), F32),
+            pltpu.VMEM((ranks, tokens // ranks, 2 * LAT), F32),
+            pltpu.VMEM((ranks, tokens // ranks, 2 * LAT), F32),
+            pltpu.VMEM((ranks, tokens // ranks, 2 * LAT), BF16),
             pltpu.VMEM((2, rows_z, 2 * tokens, HEAD_WIDTH), BF16),
             pltpu.VMEM((2, rows_z, tokens, 128), BF16),
             pltpu.VMEM((2 * rows_z, 4 * tokens, 2 * tokens), F32),
@@ -796,13 +872,13 @@
             pltpu.VMEM((window, LAT), F32),
             pltpu.VMEM((COLUMNS, quarter + 8, 128), F32),
             pltpu.VMEM((COLUMNS, quarter + 8, 128), F32),
-            pltpu.VMEM((rows_z, 16, 128), F32),
-            pltpu.VMEM((rows_z, 16, 128), F32),
-            pltpu.VMEM((quarter // 8, 8, 128), F32),
+            pltpu.VMEM((2, share_rows + 8, 128), F32),
+            pltpu.VMEM((rows_z, share_rows + 8, 128), F32),
+            pltpu.VMEM((2, share_rows + 8, 128), F32),
             pltpu.VMEM((COLUMNS, quarter, 128), F32),
         ]
         + chain * 7
-        + [dma((16,)), dma((16,)), dma((14,))],
+        + [dma((18,)), dma((18,)), dma((14,))],
         compiler_params=pltpu.CompilerParams(
             collective_id=0, has_side_effects=True, vmem_limit_bytes=60 * MIB
         ),

time: 139 us -> 137 us (0.986)
  Pallas kernels: 134 us -> 131 us
    pallas_call x1, Pallas kernels: 134 us -> 131 us  [local(): pl.pallas_call(functools.partial(kernel, rows_z), out_shape=(jax.ShapeDty...]
where the time goes in v4:
time: 137 us; the launch traced here: 135 us
  Pallas kernels  131 us (96%)
  local copies, waits for them, and re-layouts  3.21 us (2%)
    pallas_call x1, Pallas kernels, local(): pl.pallas_call(functools.partial(kernel, rows_z), out_shape=(jax.ShapeDty...  131 us
    pallas_call x2, local copies, waits for them, and re-layouts, local(): pl.pallas_call(functools.partial(kernel, rows_z), out_shape=(jax.ShapeDty...  3.21 us

profile of v4, /device:TPU:24, one launch (start us, length us, event | category | flops | bytes accessed | tf_op | source)
XLA Modules:
  0.0 135.1 jit_solution(2863935449888088544)
XLA Ops:
  1.3 130.6 %shard_map.158 = (f32[128,64]{1,0:T(8,128)}, f32[320,64]{1,0:T(8,128)}) custom-call(s32[1]{0:T(128)S(6)} %copy.19.timestep_ref, bf16[128,5120]{1,0:T(8,128)(2,1)} %student_hbm.1, f32[1,5120]{1,0:T(1,128)} %bitcast.11, bf16[64,5120]{1,0:T(8,128)(2,1)} %bitcast.7, bf16[64,128]{1,0:T(8,128)(2,1)} %bitcast.13, bf16[128,5120]{1,0:T(8,128)(2,1)} %context_hbm.1, ...), custom_call_target="tpu_custom_call" | custom-call | tf_op jit(solution)/shard_map/pallas_call | solution.py:818
  131.9 1.5 %copy.17 = f32[128,64]{0,1:T(8,128)} copy(f32[128,64]{1,0:T(8,128)} %get-tuple-element.2) | data formatting | bytes 65536 | tf_op jit(solution)/shard_map/pallas_call | solution.py:818
  133.5 1.7 %copy.18 = f32[320,64]{0,1:T(8,128)} copy(f32[320,64]{1,0:T(8,128)} %get-tuple-element.3) | data formatting | bytes 163840 | tf_op jit(solution)/shard_map/pallas_call | solution.py:818

commit v5 on v4

--- a/solution.py
+++ b/solution.py
@@ -554,31 +554,6 @@
         upper = jnp.dot(rows_at(3 - p), packed, preferred_element_type=F32)
         return lower[:, :LAT] + upper[:, LAT:]
 
-    dw.sibling_recv()
-    row = jnp.minimum(rank, rows_z - 1)
-    shift = (row * depth) % 128
-    down_placed[...] = jnp.zeros(down_placed.shape, BF16)
-    for p in range(2):
-        down_placed[p, pl.ds(pl.multiple_of(shift, 32), depth), :] = down_weights[p]
-
-    def low_term(column, p):
-        part = pl.ds(pl.multiple_of(column * span + row * depth - shift, 128), wide)
-        rows = act[:, :, part].reshape(2 * tokens, wide)
-        return jnp.dot(rows, down_placed[p], preferred_element_type=F32)
-
-    low_sum = (
-        low_term(0, 0)[:, :LAT]
-        + low_term(3, 0)[:, LAT:]
-        + low_term(1, 1)[:, :LAT]
-        + low_term(2, 1)[:, LAT:]
-    )
-    low_sum = jnp.where(rank < rows_z, low_sum, 0.0)
-    low_out[...] = jnp.concatenate([low_sum[:tokens], low_sum[tokens:]], axis=1).reshape(
-        low_out.shape
-    )
-    for k in range(1, ranks):
-        send(low_out.at[(rank + k) % ranks], low_in.at[rank], 16, fellow(k))
-    low_in[rank] = low_out[rank]
     k_product[...] = project(k_weights, pair)
     kw.sibling_recv()
     keys[pair, z] = (k_product[...] + project(k_weights, 1 - pair)).astype(BF16)
@@ -587,18 +562,46 @@
     vs = Chain(lambda p, r: values.at[p, r], v_send, v_recv, rows_z)
     ka.own()
     kb.own()
-    joined(low_in, 16, ranks - 1).wait_recv()
-    low_tiles[rank] = jnp.sum(low_in[...], axis=0).astype(BF16)
+    dw.sibling_recv()
+    row = jnp.minimum(rank, rows_z - 1)
+    shift = (row * depth) % 128
+    down_placed[...] = jnp.zeros(down_placed.shape, BF16)
+    for p in range(2):
+        down_placed[p, pl.ds(pl.multiple_of(shift, 32), depth), :] = down_weights[p]
+
+    def low_term(column, p):
+        part = pl.ds(pl.multiple_of(column * span + row * depth - shift, 128), wide)
+        rows = act[:, :, part].reshape(2 * tokens, wide)
+        return jnp.dot(rows, down_placed[p], preferred_element_type=F32)
+
+    low_sum = (
+        low_term(0, 0)[:, :LAT]
+        + low_term(3, 0)[:, LAT:]
+        + low_term(1, 1)[:, :LAT]
+        + low_term(2, 1)[:, LAT:]
+    )
+    low_sum = jnp.where(rank < rows_z, low_sum, 0.0)
+    low_out[...] = jnp.concatenate([low_sum[:tokens], low_sum[tokens:]], axis=1).reshape(
+        low_out.shape
+    )
     for k in range(1, ranks):
-        send(low_tiles.at[rank], low_tiles.at[rank], 17, fellow(k))
+        send(low_out.at[(rank + k) % ranks], low_in.at[rank], 16, fellow(k))
+    low_in[rank] = low_out[rank]
     v_product[...] = project_packed(v_weights, pair)
     vw.sibling_recv()
     moved = (v_product[...] + project_packed(v_weights, 1 - pair)).astype(BF16)
     values[pair, z] = jnp.concatenate([moved[:tokens], moved[tokens:]], axis=1)
     vs.own()
+    joined(low_in, 16, ranks - 1).wait_recv()
+    low_tiles[rank] = jnp.sum(low_in[...], axis=0).astype(BF16)
+    for k in range(1, ranks):
+        send(low_tiles.at[rank], low_tiles.at[rank], 17, fellow(k))
     q_product[...] = project(q_weights, pair)
     qw.sibling_recv()
     plain = q_product[...] + project(q_weights, 1 - pair)
+    ka.step(1)
+    kb.step(1)
+    vs.step(1)
     joined(low_tiles, 17, ranks - 1).wait_recv()
     low = low_tiles[...].reshape(tokens, 2 * LAT)
     low = jnp.concatenate([low[:, :LAT], low[:, LAT:]], axis=0)
@@ -621,9 +624,9 @@
         )
 
     def kv_steps(t, carry):
-        ka.step(t)
-        kb.step(t)
-        vs.step(t)
+        ka.step(t + 1)
+        kb.step(t + 1)
+        vs.step(t + 1)
 
         def way(d, carry):
             r = z + (1 - 2 * d) * (t - 1)
@@ -677,9 +680,14 @@
         j, target = member(k)
         send(share.at[j], met.at[me], 6, target)
     met[me] = share[me]
+    kw.drain()
+    dw.drain()
     joined(met, 6, members - 1).wait_recv()
     halves[0] = jnp.sum(met[...], axis=0)
     send(halves.at[0], halves.at[1], 7, {"grp": (1 - z_hi) * 2 + core})
+    qw.drain()
+    vw.drain()
+    ka.drain()
     joined(halves, 7, 1).wait_recv()
     shares = halves[0] + halves[1]
     taken_latent = latents[0, taken, :]
@@ -691,6 +699,7 @@
     )
     for k in range(1, ranks):
         send(tiles.at[rank], tiles.at[rank], 8, fellow(k))
+    kb.drain()
     joined(tiles, 8, ranks - 1).wait_recv()
     all_tiles = tiles[...]
     gap = jnp.sum(all_tiles, axis=0)
@@ -723,6 +732,17 @@
     for k in range(1, COLUMNS):
         other, target = in_row(k)
         send(y_out.at[other], y_in.at[y], 9, target)
+    def left(src, dst, sem):
+        copy_to(src, dst, one_send.at[sem], one_recv.at[sem], here).wait_send()
+
+    left(key_hbm.at[:, other_columns], k_weights.at[mine, z], 0)
+    left(query_hbm.at[:, other_columns], q_weights.at[mine, z], 13)
+    left(value_hbm.at[:, other_columns], value_mail, 1)
+    left(down_hbm, down_mail, 14)
+    joined(low_out, 16, ranks - 1).wait_send()
+    joined(low_tiles, 17, ranks - 1).wait_send()
+    left(act.at[side, this_half], act.at[side, this_half], 5)
+    left(act.at[1 - side, this_half], act.at[1 - side, this_half], 15)
     y_in[y] = y_out[y]
     joined(y_in, 9, COLUMNS - 1).wait_recv()
     sums = jnp.sum(y_in[...], axis=0)
@@ -737,6 +757,9 @@
         z_out[o, share_rows : share_rows + 8, :] = sums[quarter:]
     to_owners(z_out, z_in, 10)
     token_scale = float(tokens * seqs) ** -0.5
+    vs.drain()
+    joined(fold_column, 2, COLUMNS - 1).wait_send()
+    owners_left(fold_rows, fold_arrived, fold_whole, 3, 4)
 
     @pl.when(is_owner)
     def _():
@@ -760,27 +783,12 @@
     grad_ref[0 : grad_rows // 2, :] = complete[:, :LAT]
     grad_ref[grad_rows // 2 :, :] = complete[:, LAT:]
 
-    def left(src, dst, sem):
-        copy_to(src, dst, one_send.at[sem], one_recv.at[sem], here).wait_send()
-
-    left(key_hbm.at[:, other_columns], k_weights.at[mine, z], 0)
-    left(query_hbm.at[:, other_columns], q_weights.at[mine, z], 13)
-    left(value_hbm.at[:, other_columns], value_mail, 1)
-    left(down_hbm, down_mail, 14)
-    joined(low_out, 16, ranks - 1).wait_send()
-    joined(low_tiles, 17, ranks - 1).wait_send()
-    left(act.at[side, this_half], act.at[side, this_half], 5)
-    left(act.at[1 - side, this_half], act.at[1 - side, this_half], 15)
-    joined(fold_column, 2, COLUMNS - 1).wait_send()
-    owners_left(fold_rows, fold_arrived, fold_whole, 3, 4)
     joined(share, 6, members - 1).wait_send()
     joined(halves, 7, 1).wait_send()
     joined(tiles, 8, ranks - 1).wait_send()
     joined(y_out, 9, COLUMNS - 1).wait_send()
     owners_left(z_out, z_in, pieces, 10, 11)
     joined(columns, 12, COLUMNS - 1).wait_send()
-    for chain in (kw, qw, vw, dw, ka, kb, vs):
-        chain.drain()
 
 
 def local(

time: 137 us -> 133 us (0.971)
  Pallas kernels: 131 us -> 127 us
    pallas_call x1, Pallas kernels: 131 us -> 127 us  [local(): pl.pallas_call(functools.partial(kernel, rows_z), out_shape=(jax.ShapeDty...]
where the time goes in v5:
time: 133 us; the launch traced here: 131 us
  Pallas kernels  127 us (95%)
  local copies, waits for them, and re-layouts  3.21 us (2%)
    pallas_call x1, Pallas kernels, local(): pl.pallas_call(functools.partial(kernel, rows_z), out_shape=(jax.ShapeDty...  127 us
    pallas_call x2, local copies, waits for them, and re-layouts, local(): pl.pallas_call(functools.partial(kernel, rows_z), out_shape=(jax.ShapeDty...  3.21 us

profile of v5, /device:TPU:24, one launch (start us, length us, event | category | flops | bytes accessed | tf_op | source)
XLA Modules:
  0.0 131.1 jit_solution(14489724874909698670)
XLA Ops:
  1.3 126.6 %shard_map.158 = (f32[128,64]{1,0:T(8,128)}, f32[320,64]{1,0:T(8,128)}) custom-call(s32[1]{0:T(128)S(6)} %copy.19.timestep_ref, bf16[128,5120]{1,0:T(8,128)(2,1)} %student_hbm.1, f32[1,5120]{1,0:T(1,128)} %bitcast.11, bf16[64,5120]{1,0:T(8,128)(2,1)} %bitcast.7, bf16[64,128]{1,0:T(8,128)(2,1)} %bitcast.13, bf16[128,5120]{1,0:T(8,128)(2,1)} %context_hbm.1, ...), custom_call_target="tpu_custom_call" | custom-call | tf_op jit(solution)/shard_map/pallas_call | solution.py:826
  127.9 1.5 %copy.17 = f32[128,64]{0,1:T(8,128)} copy(f32[128,64]{1,0:T(8,128)} %get-tuple-element.2) | data formatting | bytes 65536 | tf_op jit(solution)/shard_map/pallas_call | solution.py:826
  129.4 1.7 %copy.18 = f32[320,64]{0,1:T(8,128)} copy(f32[320,64]{1,0:T(8,128)} %get-tuple-element.3) | data formatting | bytes 163840 | tf_op jit(solution)/shard_map/pallas_call | solution.py:826

commit v6 on v5

--- a/solution.py
+++ b/solution.py
@@ -636,20 +636,23 @@
             def _():
                 score_unit(pair, r)
 
+            far = z + (1 - 2 * d) * (t - 2)
+            near = jnp.logical_and(t == 2, d == 0)
+            held = jnp.logical_and(far >= 0, far < rows_z)
+
+            @pl.when(jnp.logical_and(held, jnp.logical_or(t > 2, near)))
+            def _():
+                ka.copy(1 - pair, far, 2, sibling).wait_recv()
+                kb.copy(1 - pair, far, 2, sibling).wait_recv()
+                score_unit(1 - pair, far)
+
             return carry
 
         lax.fori_loop(0, 2, way, 0)
         return carry
 
-    lax.fori_loop(1, rows_z + 1, kv_steps, 0)
-
-    def from_sibling(r, carry):
-        ka.copy(1 - pair, r, 2, sibling).wait_recv()
-        kb.copy(1 - pair, r, 2, sibling).wait_recv()
-        score_unit(1 - pair, r)
-        return carry
-
-    lax.fori_loop(0, rows_z, from_sibling, 0)
+    lax.fori_loop(1, rows_z + 2, kv_steps, 0)
+
     vs.sibling_recv()
     peak = jnp.max(top[...], axis=-1, keepdims=True)
     top[...] = jnp.broadcast_to(peak, top.shape)

time: 133 us -> 133 us (level)
  no operation moved by 1% of the time
where the time goes in v6:
time: 133 us; the launch traced here: 131 us
  Pallas kernels  126 us (95%)
  local copies, waits for them, and re-layouts  3.21 us (2%)
    pallas_call x1, Pallas kernels, local(): pl.pallas_call(functools.partial(kernel, rows_z), out_shape=(jax.ShapeDty...  126 us
    pallas_call x2, local copies, waits for them, and re-layouts, local(): pl.pallas_call(functools.partial(kernel, rows_z), out_shape=(jax.ShapeDty...  3.21 us

profile of v6, /device:TPU:24, one launch (start us, length us, event | category | flops | bytes accessed | tf_op | source)
XLA Modules:
  0.0 130.7 jit_solution(7369491707768549269)
XLA Ops:
  1.3 126.2 %shard_map.158 = (f32[128,64]{1,0:T(8,128)}, f32[320,64]{1,0:T(8,128)}) custom-call(s32[1]{0:T(128)S(6)} %copy.19.timestep_ref, bf16[128,5120]{1,0:T(8,128)(2,1)} %student_hbm.1, f32[1,5120]{1,0:T(1,128)} %bitcast.11, bf16[64,5120]{1,0:T(8,128)(2,1)} %bitcast.7, bf16[64,128]{1,0:T(8,128)(2,1)} %bitcast.13, bf16[128,5120]{1,0:T(8,128)(2,1)} %context_hbm.1, ...), custom_call_target="tpu_custom_call" | custom-call | tf_op jit(solution)/shard_map/pallas_call | solution.py:829
  127.5 1.5 %copy.17 = f32[128,64]{0,1:T(8,128)} copy(f32[128,64]{1,0:T(8,128)} %get-tuple-element.2) | data formatting | bytes 65536 | tf_op jit(solution)/shard_map/pallas_call | solution.py:829
  129.1 1.7 %copy.18 = f32[320,64]{0,1:T(8,128)} copy(f32[320,64]{1,0:T(8,128)} %get-tuple-element.3) | data formatting | bytes 163840 | tf_op jit(solution)/shard_map/pallas_call | solution.py:829
